TPU v7x, 32 devices: a whole 2x2x4 slice. The times are simulated.
32 devices in a mesh: img: 8 (over z, x), txt: 4 (over y, core).
Axes of the slice: x: 2, y: 2, z: 4, core: 2. Of those that a mesh axis runs over, the one named last changes fastest.
Arguments:
- image_tokens: bfloat16 [4096, 256], P(('img', 'txt')), may hold values from -6 to 6
- prompt_tokens: bfloat16 [768, 256], P(('txt', 'img')), may hold values from -6 to 6
- category_ids: int32 [768], P(('txt', 'img')), may hold values from 0 to 47, as said below
- prompt_valid: int32 [768], P(('txt', 'img')), may hold values from 0 to 1, as said below
- image_gain: float32 [256], replicated, may hold values from 0.5 to 1.5
- prompt_gain: float32 [256], replicated, may hold values from 0.5 to 1.5
- query_weight: bfloat16 [256, 1024], replicated, may hold values from -1.7 to 1.7
- key_weight: bfloat16 [256, 1024], replicated, may hold values from -1.7 to 1.7
- image_value_weight: bfloat16 [256, 1024], replicated, may hold values from -0.375 to 0.375
- prompt_value_weight: bfloat16 [256, 1024], replicated, may hold values from -0.375 to 0.375
- image_out_weight: bfloat16 [1024, 256], replicated, may hold values from -0.1875 to 0.1875
- prompt_out_weight: bfloat16 [1024, 256], replicated, may hold values from -0.1875 to 0.1875
- image_layer_scale: float32 [256], replicated, may hold values from 1 to 4
- prompt_layer_scale: float32 [256], replicated, may hold values from 1 to 4
Outputs:
- joined_image: bfloat16 [4096, 256], P(('img', 'txt'))
- joined_prompt: bfloat16 [768, 256], P(('txt', 'img'))
- category_embed: float32 [48, 256], replicated
Inputs may be any that keep to these rules, and one draw needn't show every extreme that they name: `category_ids`: along the prompt the ids never fall; each of the 48 categories holds between 4 and 28 consecutive tokens. `prompt_valid`: within each category the tokens marked 1 come first, and at least one token is marked 1.
All inputs are finite; a program needn't handle non-finite values.
Results may differ from a plain program's by a relative error of at most 0.009.
The roundings to bfloat16 on the way count: a program that leaves them out, or rounds other values in their place, can miss the bound.
Values may be sent and summed in bfloat16 or wider, within the bound.
A program may use at most 128 MiB of HBM per device.

v0:
```python
import math

import jax
import jax.numpy as jnp
from jax import lax
from jax.sharding import PartitionSpec as P

HD = 256


EPSILON = 1e-05
MASKED = -1e30


def normalize(tokens_in, gain_row):
    values = tokens_in.astype(jnp.float32)
    average = jnp.mean(values, axis=-1, keepdims=True)
    centered = values - average
    variance = jnp.mean(centered * centered, axis=-1, keepdims=True)
    return (centered * lax.rsqrt(variance + EPSILON) * gain_row).astype(jnp.bfloat16)


def on_device(
    image_tokens,
    prompt_tokens,
    category_ids,
    prompt_valid,
    image_gain,
    prompt_gain,
    query_weight,
    key_weight,
    image_value_weight,
    prompt_value_weight,
    image_out_weight,
    prompt_out_weight,
    image_layer_scale,
    prompt_layer_scale,
):
    embed_width = query_weight.shape[1]
    head_count = embed_width // HD
    image_normed = normalize(image_tokens, image_gain)
    image_weights = jnp.concatenate([query_weight, image_value_weight], axis=1)
    image_projected = jnp.dot(
        lax.all_gather(image_normed, "txt", axis=0, tiled=True),
        image_weights,
        preferred_element_type=jnp.float32,
    ).astype(jnp.bfloat16)
    prompt_normed = normalize(prompt_tokens, prompt_gain)
    prompt_weights = jnp.concatenate([key_weight, prompt_value_weight], axis=1)
    valid_marks = prompt_valid.astype(jnp.bfloat16)
    gathered, marks_all = (
        lax.all_gather(prompt_normed, "img", axis=0, tiled=True),
        lax.all_gather(valid_marks, "img", axis=0, tiled=True),
    )
    prompt_projected = jnp.dot(gathered, prompt_weights, preferred_element_type=jnp.float32).astype(
        jnp.bfloat16
    )
    image_count = image_projected.shape[0]
    prompt_count = prompt_projected.shape[0]
    query_heads = image_projected[:, :embed_width].reshape(image_count, head_count, HD)
    image_value_heads = image_projected[:, embed_width:].reshape(image_count, head_count, HD)
    key_heads = prompt_projected[:, :embed_width].reshape(prompt_count, head_count, HD)
    prompt_value_heads = prompt_projected[:, embed_width:].reshape(prompt_count, head_count, HD)
    scores = jnp.einsum(
        "ihd,thd->hit", query_heads, key_heads, preferred_element_type=jnp.float32
    ) / math.sqrt(HD)
    is_valid = (marks_all > 0)[None, None, :]
    masked = jnp.where(is_valid, scores, MASKED)
    row_top = lax.pmax(jnp.max(masked, axis=2), "txt")
    col_top = lax.pmax(jnp.max(scores, axis=1), "img")
    row_exp = jnp.where(is_valid, jnp.exp(masked - row_top[:, :, None]), 0.0)
    col_exp = jnp.exp(scores - col_top[:, None, :])
    row_sum = lax.psum(jnp.sum(row_exp, axis=2), "txt")
    col_sum = lax.psum(jnp.sum(col_exp, axis=1), "img")
    row_weights = row_exp.astype(jnp.bfloat16)
    col_weights = col_exp.astype(jnp.bfloat16)
    image_numer = jnp.einsum(
        "hit,thd->ihd", row_weights, prompt_value_heads, preferred_element_type=jnp.float32
    )
    image_part = (
        (image_numer / row_sum.T[:, :, None]).reshape(image_count, embed_width).astype(jnp.bfloat16)
    )
    block_rows = image_part
    image_delta = lax.psum_scatter(
        jnp.dot(block_rows, image_out_weight, preferred_element_type=jnp.float32).astype(
            jnp.bfloat16
        ),
        "txt",
        scatter_dimension=0,
        tiled=True,
    ).astype(jnp.float32)
    joined_image = (image_tokens.astype(jnp.float32) + image_layer_scale * image_delta).astype(
        jnp.bfloat16
    )
    prompt_numer = jnp.einsum(
        "hit,ihd->thd", col_weights, image_value_heads, preferred_element_type=jnp.float32
    )
    prompt_part = (
        (prompt_numer / col_sum.T[:, :, None])
        .reshape(prompt_count, embed_width)
        .astype(jnp.bfloat16)
    )
    block_rows = prompt_part
    prompt_delta = lax.psum_scatter(
        jnp.dot(block_rows, prompt_out_weight, preferred_element_type=jnp.float32),
        "img",
        scatter_dimension=0,
        tiled=True,
    )
    prompt_joined = prompt_tokens.astype(jnp.float32) + prompt_layer_scale * prompt_delta
    category_count = prompt_count * lax.axis_size("txt") // 16
    members = jnp.logical_and(
        category_ids[None, :] == jnp.arange(category_count, dtype=jnp.int32)[:, None],
        prompt_valid[None, :] > 0,
    ).astype(jnp.float32)
    category_sum = jnp.dot(members, prompt_joined, precision=lax.Precision.HIGHEST)
    category_tally = jnp.sum(members, axis=1)
    category_sum, category_tally = lax.psum((category_sum, category_tally), ("img", "txt"))
    category_embed = category_sum / category_tally[:, None]
    return (joined_image, prompt_joined.astype(jnp.bfloat16), category_embed)


def solution(mesh):
    return jax.shard_map(
        on_device,
        mesh=mesh,
        in_specs=(
            P(("img", "txt"), None),
            P(("txt", "img"), None),
            P(("txt", "img")),
            P(("txt", "img")),
            P(),
            P(),
            P(),
            P(),
            P(),
            P(),
            P(),
            P(),
            P(),
            P(),
        ),
        out_specs=(P(("img", "txt"), None), P(("txt", "img"), None), P()),
        check_vma=False,
    )
```

profile of v0, /device:TPU:0, one launch (start us, length us, event | category | flops | bytes accessed | tf_op | source)
XLA Modules:
  0.0 237.2 jit_solution(6789057603095514729)
XLA Ops:
  7.2 1.0 convert_reduce_fusion
  8.2 1.0 fusion.31
  9.3 1.0 fusion.33
  10.2 7.2 %all_gather.11 = bf16[512,256]{1,0:T(8,128)(2,1)S(1)} all-gather(bf16[128,256]{1,0:T(8,128)(2,1)S(1)} %fusion.33), channel_id=1, replica_groups=mesh['img'=8,'txt'=4] {'txt'}, dimensions={0}, use_global_device_ids=true | all-gather | bytes 327680 | tf_op jit(solution)/shard_map/all_gather | solution.py:44
  17.5 1.9 convolution_convert_fusion
  19.4 1.2 fusion.52
  20.6 0.1 convert_reduce_fusion.1
  20.7 0.2 fusion.37
  20.9 0.1 fusion.39
  21.0 30.9 %all_gather.9 = bf16[192,256]{1,0:T(8,128)(2,1)S(1)} all-gather(bf16[24,256]{1,0:T(8,128)(2,1)S(1)} %fusion.39), channel_id=1, replica_groups=mesh['img'=8,'txt'=4] {'img'}, dimensions={0}, use_global_device_ids=true | all-gather | bytes 110592 | tf_op jit(solution)/shard_map/all_gather | solution.py:52
  51.9 0.4 convolution_convert_fusion.1
  52.3 0.8 fusion.53
  53.1 0.6 dynamic-slice
  54.4 0.2 dynamic-update-slice
  54.6 21.3 %all-reduce = bf16[192]{0:T(256)(128)(2,1)S(1)} all-reduce(bf16[192]{0:T(256)(128)(2,1)S(1)} %dynamic-update-slice), channel_id=1, replica_groups=mesh['img'=8,'txt'=4] {'img'}, use_global_device_ids=true, to_apply=%add | all-reduce | flops 192 | bytes 768
  75.9 2.5 %fusion.51 = (f32[4,192]{1,0:T(4,128)}, f32[4,512]{1,0:T(4,128)}, f32[4,512,192]{1,2,0:T(8,128)S(1)}) fusion(pred[192]{0:T(512)(128)(4,1)S(1)} %broadcast_compare_fusion, bf16[24,4,8,256]{3,2,1,0:T(8,128)(2,1)} %bitcast.49, bf16[64,4,8,256]{3,2,1,0:T(8,128)(2,1)} %bitcast.47), kind=kOutput, calls=%fused_computation.72 | convolution fusion | flops 202896640 | bytes 3026112 | tf_op jit(solution)/shard_map/ihd,thd->hit/dot_general | solution.py:64
  78.5 6.4 %pmax.14 = f32[4,512]{1,0:T(4,128)} all-reduce(f32[4,512]{1,0:T(4,128)} %get-tuple-element.6), channel_id=1, replica_groups=mesh['img'=8,'txt'=4] {'txt'}, use_global_device_ids=true, to_apply=%region_5.6 | all-reduce | flops 2048 | bytes 16384 | tf_op jit(solution)/shard_map/pmax | solution.py:69
  84.9 17.2 %pmax.15 = f32[4,192]{1,0:T(4,128)S(1)} all-reduce(f32[4,192]{1,0:T(4,128)} %get-tuple-element.5), channel_id=1, replica_groups=mesh['img'=8,'txt'=4] {'img'}, use_global_device_ids=true, to_apply=%region_10.11 | all-reduce | flops 768 | bytes 6144 | tf_op jit(solution)/shard_map/pmax | solution.py:70
  102.1 2.1 fusion.1
  104.2 19.8 %psum.29 = f32[192,4]{0,1:T(4,128)} all-reduce(f32[192,4]{0,1:T(4,128)} %bitcast.51), channel_id=1, replica_groups=mesh['img'=8,'txt'=4] {'img'}, use_global_device_ids=true, to_apply=%region_12.13 | all-reduce | flops 768 | bytes 6144 | tf_op jit(solution)/shard_map/psum | solution.py:74
  124.1 1.3 fusion.5
  125.4 1.0 fusion.54
  126.4 5.8 %psum.28 = f32[512,4]{0,1:T(4,128)S(1)} all-reduce(f32[512,4]{0,1:T(4,128)S(1)} %bitcast.50), channel_id=1, replica_groups=mesh['img'=8,'txt'=4] {'txt'}, use_global_device_ids=true, to_apply=%region_7.8 | all-reduce | flops 2048 | bytes 16384 | tf_op jit(solution)/shard_map/psum | solution.py:73
  132.2 0.7 fusion
  133.0 1.2 convolution_convert_fusion.2
  134.2 0.1 convert_reduce_fusion.2
  134.3 50.8 %reduce-scatter.5.cloned.1.call-done = f32[24,256]{1,0:T(8,128)} async-done(((f32[192,256]{1,0:T(8,128)}), f32[24,256]{1,0:T(8,128)}) %reduce-scatter.5.cloned.1.call-update) | async-done | bytes 24592 | tf_op jit(solution)/shard_map/reduce_scatter | solution.py:104
  185.1 1.0 fusion.40
  186.1 40.6 %all-reduce.1 = (f32[48,256]{1,0:T(8,128)S(1)}, f32[48]{0:T(128)S(1)}) all-reduce(f32[48,256]{1,0:T(8,128)S(1)} %fusion.40, f32[48]{0:T(128)S(1)} %convert_reduce_fusion.2), channel_id=1, replica_groups=mesh['img'=8,'txt'=4] {'img','txt'}, use_global_device_ids=true, to_apply=%region_14.15 | all-reduce | flops 12336 | bytes 98688 | tf_op jit(solution)/shard_map/psum | solution.py:118
  226.8 1.3 fusion.41
  228.1 0.7 broadcast_divide_fusion
  228.8 1.5 fusion.34
  (48 shorter events, 0.3 us)
Async XLA Ops:
  7.2 125.8 %copy-start = (bf16[1024,256]{1,0:T(8,128)(2,1)S(1)}, bf16[1024,256]{1,0:T(8,128)(2,1)}, u32[]{:S(2)}) copy-start(bf16[1024,256]{1,0:T(8,128)(2,1)} %param.24) | copy-start | bytes 1572868
  7.2 177.9 %reduce-scatter.5.cloned.1.call-start = ((), (), s32[]{:S(2)}) async-start(), calls=%async_computation.3 | async-start | bytes 221184 | tf_op jit(solution)/shard_map/reduce_scatter | solution.py:104
  19.4 1.2 copy-start.3
  19.4 1.5 copy-start.8
  19.4 32.5 %copy-start.11 = (bf16[256,1024]{1,0:T(8,128)(2,1)S(1)}, bf16[256,1024]{1,0:T(8,128)(2,1)}, u32[]{:S(2)}) copy-start(bf16[256,1024]{1,0:T(8,128)(2,1)} %param.23) | copy-start | bytes 1572868
  19.4 32.5 %copy-start.12 = (bf16[256,1024]{1,0:T(8,128)(2,1)S(1)}, bf16[256,1024]{1,0:T(8,128)(2,1)}, u32[]{:S(2)}) copy-start(bf16[256,1024]{1,0:T(8,128)(2,1)} %param.21) | copy-start | bytes 1572868
  51.9 1.2 copy-start.13
  51.9 1.2 copy-start.16
  75.9 2.5 %copy-start.9 = (pred[192]{0:T(512)(128)(4,1)}, pred[192]{0:T(512)(128)(4,1)S(1)}, u32[]{:S(2)}) copy-start(pred[192]{0:T(512)(128)(4,1)S(1)} %broadcast_compare_fusion) | copy-start | bytes 580
  124.1 1.3 copy-start.2
  125.3 1.1 copy-start.5
  125.3 6.9 %copy-start.4 = (f32[4,512]{1,0:T(4,128)S(1)}, f32[4,512]{1,0:T(4,128)}, u32[]{:S(2)}) copy-start(f32[4,512]{1,0:T(4,128)} %pmax.14) | copy-start | bytes 24580
  125.3 6.9 %copy-start.10 = (pred[192]{0:T(512)(128)(4,1)S(1)}, pred[192]{0:T(512)(128)(4,1)}, u32[]{:S(2)}) copy-start(pred[192]{0:T(512)(128)(4,1)} %copy-done.9) | copy-start | bytes 580
  126.4 102.4 %reduce-scatter.3.cloned.1.call-start = ((), (), s32[]{:S(2)}) async-start(), calls=%async_computation.2 | async-start | bytes 327680 | tf_op jit(solution)/shard_map/reduce_scatter | solution.py:84
  132.9 1.3 copy-start.14
  132.9 1.3 copy-start.15
  132.9 52.2 %copy-start.7 = (f32[256]{0:T(256)S(1)}, f32[256]{0:T(256)}, u32[]{:S(2)}) copy-start(f32[256]{0:T(256)} %param.27) | copy-start | bytes 3076
  132.9 95.9 %copy-start.1 = (bf16[128,256]{1,0:T(8,128)(2,1)S(1)}, bf16[128,256]{1,0:T(8,128)(2,1)}, u32[]{:S(2)}) copy-start(bf16[128,256]{1,0:T(8,128)(2,1)} %param.14) | copy-start | bytes 196612
  133.0 95.9 %copy-start.6 = (f32[256]{0:T(256)S(1)}, f32[256]{0:T(256)}, u32[]{:S(2)}) copy-start(f32[256]{0:T(256)} %param.26) | copy-start | bytes 3076
Sparse Core Ops, SparseCore 0:
  126.5 58.5 reduce-scatter.4
  187.5 19.0 reduce-scatter.2
where the time goes:
time: 238 us; the launch traced here: 237 us
  blocking collectives  149 us (63%)
  waiting for transfers between devices  50.8 us (21%)
  between operations  15 us (6%)
  matrix products  9.92 us (4%)
  other arithmetic  9.08 us (4%)
  local copies, waits for them, and re-layouts  2.93 us (1%)
    reduce_scatter x1, waiting for transfers between devices, on_device(): lax.psum_scatter(jnp.dot(block_rows, prompt_out_weight, preferred_element...  50.8 us
    psum x1, blocking collectives, on_device(): lax.psum((category_sum, category_tally), ('img', 'txt'))  40.6 us
    all_gather x1, blocking collectives, on_device(): lax.all_gather(prompt_normed, 'img', axis=0, tiled=True)  30.9 us
    unnamed x1, blocking collectives  21.3 us
    psum x1, blocking collectives, on_device(): col_sum = lax.psum(jnp.sum(col_exp, axis=1), 'img')  19.8 us
    pmax x1, blocking collectives, on_device(): col_top = lax.pmax(jnp.max(scores, axis=1), 'img')  17.2 us
    all_gather x1, blocking collectives, on_device(): lax.all_gather(image_normed, 'txt', axis=0, tiled=True)  7.22 us
    pmax x1, blocking collectives, on_device(): row_top = lax.pmax(jnp.max(masked, axis=2), 'txt')  6.44 us
  transfers between devices with their start and end apart: 2, of which 1 were waited for; matrix products, arithmetic and copies ran while one was open for 2% of the time, Pallas kernels for 0%

commit v1 on v0

v1 whole, which is shorter than its diff:
```python
import functools

import jax
import jax.numpy as jnp
from jax import lax
from jax.experimental import pallas as pl
from jax.experimental.pallas import tpu as pltpu
from jax.sharding import PartitionSpec as P

HD = 256
EPSILON = 1e-05
MASKED = -1e30
FLOOR = -1e29
WINDOW = 8
COUNT_BASE = 4096
MESH = pl.DeviceIdType.MESH
F32 = jnp.float32
BF16 = jnp.bfloat16


def normalize(tokens_in, gain_row):
    values = tokens_in.astype(F32)
    average = jnp.mean(values, axis=-1, keepdims=True)
    centered = values - average
    variance = jnp.mean(centered * centered, axis=-1, keepdims=True)
    return centered * lax.rsqrt(variance + EPSILON) * gain_row


def iota(shape, dim):
    return lax.broadcasted_iota(jnp.int32, shape, dim)


def mm(a, b):
    return jnp.dot(a, b, preferred_element_type=F32)


def mm_t(a, b):
    return lax.dot_general(a, b, (((1,), (1,)), ((), ())), preferred_element_type=F32)


def kernel(
    n_img, n_txt,
    img_ref, prompt_ref, ids_ref, valid_ref, igain_ref, pgain_ref,
    wq_hbm, wk_hbm, wvi_hbm, wvp_hbm, woi_hbm, wop_hbm, iscale_ref, pscale_ref,
    out_img, out_prompt, out_cat,
    wq, wk, wvi, wvp, woi, wop, xi, xp, meta, numer_i, numer_p, stat_r, stat_c,
    di_out, di_in, dp_out, dp_in, win,
    w_sem, xi_s, xi_r, xp_s, xp_r, meta_s, meta_r, sr_s, sr_r, sc_s, sc_r,
    di_s, di_r, dp_s, dp_r, win_s, win_r,
):
    n_dev = n_img * n_txt
    my_img, my_txt = lax.axis_index("img"), lax.axis_index("txt")
    me = my_img * n_txt + my_txt
    rows, width = img_ref.shape
    tokens = prompt_ref.shape[0]
    padded = xp.shape[1]
    embed = wq.shape[1]
    heads = embed // HD
    n_rows = n_txt * rows
    n_cols = n_img * padded

    weights = ((wk_hbm, wk), (wvp_hbm, wvp), (wq_hbm, wq), (wvi_hbm, wvi), (wop_hbm, wop), (woi_hbm, woi))
    loads = [pltpu.make_async_copy(src, dst, w_sem.at[n]) for n, (src, dst) in enumerate(weights)]
    for load in loads:
        load.start()

    barrier = pltpu.get_barrier_semaphore()

    def device(d):
        return {"img": d // n_txt, "txt": d % n_txt}

    @pl.loop(1, n_dev)
    def _(step):
        pl.semaphore_signal(barrier, inc=1, device_id=device(lax.rem(me + step, n_dev)), device_id_type=MESH)

    normed = normalize(prompt_ref[...], pgain_ref[...].reshape(1, width))
    valid_row = valid_ref[...].reshape(1, tokens)
    ids_row = ids_ref[...].reshape(1, tokens)
    diagonal = iota((tokens, tokens), 0) == iota((tokens, tokens), 1)
    valid_col = jnp.sum(jnp.where(diagonal, jnp.broadcast_to(valid_row, (tokens, tokens)).astype(F32), 0.0), axis=1, keepdims=True)
    place = my_img * padded
    spot = place % width + iota((tokens, width), 0) == iota((tokens, width), 1)
    mark_row = jnp.sum(jnp.where(spot, valid_col, 0.0), axis=0, keepdims=True)
    spare = padded - tokens
    marks = jnp.where(iota((spare, width), 0) == place // width, mark_row, 0.0)
    xp[my_img] = jnp.concatenate([normed, marks], axis=0).astype(BF16)

    rel = ids_row - ids_row[:, 0:1]
    members = jnp.logical_and(rel == iota((WINDOW, tokens), 0), valid_row > 0).astype(F32)
    counts = jnp.sum(members, axis=1, keepdims=True).astype(jnp.int32)
    lane = iota((WINDOW, 128), 1) - (me % 8) * 16
    slot = iota((WINDOW, 128), 0)
    mine = jnp.logical_and(jnp.logical_and(lane >= 0, lane < 16), lane % WINDOW == slot)
    value = counts * COUNT_BASE + ids_row[:, 0:1] + slot
    meta[me] = jnp.sum(jnp.where(mine, value, 0), axis=0, keepdims=True)

    xi[my_txt] = normalize(img_ref[...], igain_ref[...].reshape(1, width)).astype(BF16)

    def over_img(src, dst, s, r, p, to=None):
        return pltpu.make_async_remote_copy(src, dst, s.at[p], r.at[my_img], device_id={"img": p, "txt": my_txt}, device_id_type=MESH)

    def over_txt(src, dst, s, r, p):
        return pltpu.make_async_remote_copy(src, dst, s.at[p], r.at[my_txt], device_id={"img": my_img, "txt": p}, device_id_type=MESH)

    def gather_copy(buf, s, r, axis, p):
        mine_ = my_img if axis == "img" else my_txt
        make = over_img if axis == "img" else over_txt
        return make(buf.at[mine_], buf.at[mine_], s, r, p)

    def scatter_copy(out, into, s, r, axis, p):
        mine_ = my_img if axis == "img" else my_txt
        make = over_img if axis == "img" else over_txt
        return make(out.at[p], into.at[mine_], s, r, p)

    def arrived(buf, s, r, p):
        pltpu.make_async_remote_copy(buf.at[p], buf.at[p], s.at[p], r.at[p], device_id={"img": my_img, "txt": my_txt}, device_id_type=MESH).wait_recv()

    def others(axis, body):
        count, mine_ = (n_img, my_img) if axis == "img" else (n_txt, my_txt)

        @pl.loop(1, count)
        def _(step):
            body(lax.rem(mine_ + step, count))

    def everyone(body):
        @pl.loop(1, n_dev)
        def _(step):
            body(lax.rem(me + step, n_dev))

    def wide(buf, s, r, p):
        return pltpu.make_async_remote_copy(buf.at[me], buf.at[me], s.at[p], r.at[me], device_id=device(p), device_id_type=MESH)

    pl.semaphore_wait(barrier, n_dev - 1)

    others("txt", lambda p: gather_copy(xi, xi_s, xi_r, "txt", p).start())
    others("img", lambda p: gather_copy(xp, xp_s, xp_r, "img", p).start())
    everyone(lambda p: wide(meta, meta_s, meta_r, p).start())

    for load in loads[:4]:
        load.wait()
    others("img", lambda p: arrived(xp, xp_s, xp_r, p))
    others("txt", lambda p: arrived(xi, xi_s, xi_r, p))

    x_prompt = xp[...].reshape(n_cols, width)
    x_image = xi[...].reshape(n_rows, width)
    mark_rows = jnp.sum(xp[:, tokens:, :].astype(F32), axis=0)
    mask = jnp.concatenate([mark_rows[n : n + 1] for n in range(max(1, n_cols // width))], axis=1)[:, :n_cols] > 0.0

    def one_head(h, carry):
        row_stats, col_stats = carry
        part = pl.ds(pl.multiple_of(h * HD, HD), HD)
        k = mm(x_prompt, wk[:, part]).astype(BF16)
        q = (mm(x_image, wq[:, part]) * (HD ** -0.5)).astype(BF16)
        v_p = mm(x_prompt, wvp[:, part]).astype(BF16)
        v_i = mm(x_image, wvi[:, part]).astype(BF16)
        turned = mm_t(k, q)
        c_top = jnp.max(turned, axis=1, keepdims=True)
        c_exp = jnp.exp(turned - c_top)
        c_sum = jnp.sum(c_exp, axis=1, keepdims=True)
        numer_p[h] = mm(c_exp.astype(BF16), v_i)
        scores = jnp.where(mask, mm_t(q, k), MASKED)
        r_top = jnp.maximum(jnp.max(scores, axis=1, keepdims=True), FLOOR)
        r_exp = jnp.exp(scores - r_top)
        r_sum = jnp.sum(r_exp, axis=1, keepdims=True)
        numer_i[h] = mm(r_exp.astype(BF16), v_p)

        def put(stats, top, total):
            at = iota(stats.shape, 1)
            return jnp.where(at == h, top, jnp.where(at == heads + h, total, stats))

        return put(row_stats, r_top, r_sum), put(col_stats, c_top, c_sum)

    carry = (jnp.zeros((n_rows, 128), F32), jnp.zeros((n_cols, 128), F32))
    if n_cols <= 512:
        for h in range(heads):
            carry = one_head(h, carry)
    else:
        carry = lax.fori_loop(0, heads, one_head, carry)
    row_stats, col_stats = carry
    stat_c[my_img] = col_stats.T[: 2 * heads]
    others("img", lambda p: gather_copy(stat_c, sc_s, sc_r, "img", p).start())
    stat_r[my_txt] = row_stats.T[: 2 * heads]
    others("txt", lambda p: gather_copy(stat_r, sr_s, sr_r, "txt", p).start())

    def factor(buf, mine_):
        tops, sums = buf[:, :heads, :], buf[:, heads:, :]
        top = jnp.max(tops, axis=0)
        total = jnp.sum(sums * jnp.exp(tops - top[None]), axis=0)
        own = jnp.exp(buf[mine_][:heads] - top) / total
        return jnp.concatenate([own, jnp.zeros((128 - heads, own.shape[1]), F32)], axis=0).T

    for load in loads[4:]:
        load.wait()
    others("img", lambda p: arrived(stat_c, sc_s, sc_r, p))
    scale = factor(stat_c, my_img)
    delta = mm((numer_p[0] * scale[:, 0:1]).astype(BF16), wop[0:HD, :])
    for h in range(1, heads):
        delta += mm((numer_p[h] * scale[:, h : h + 1]).astype(BF16), wop[h * HD : (h + 1) * HD, :])
    dp_out[...] = delta.astype(BF16).reshape(dp_out.shape)
    dp_in[my_img] = dp_out[my_img]
    others("img", lambda p: scatter_copy(dp_out, dp_in, dp_s, dp_r, "img", p).start())

    others("txt", lambda p: arrived(stat_r, sr_s, sr_r, p))
    scale = factor(stat_r, my_txt)
    delta = mm((numer_i[0] * scale[:, 0:1]).astype(BF16), woi[0:HD, :])
    for h in range(1, heads):
        delta += mm((numer_i[h] * scale[:, h : h + 1]).astype(BF16), woi[h * HD : (h + 1) * HD, :])
    di_out[...] = delta.astype(BF16).reshape(di_out.shape)
    di_in[my_txt] = di_out[my_txt]
    others("txt", lambda p: scatter_copy(di_out, di_in, di_s, di_r, "txt", p).start())

    others("img", lambda p: arrived(dp_in, dp_s, dp_r, p))
    prompt_delta = jnp.sum(dp_in[...].astype(F32), axis=0)[:tokens]
    joined = prompt_ref[...].astype(F32) + pscale_ref[...].reshape(1, width) * prompt_delta
    out_prompt[...] = joined.astype(BF16)
    sums = jnp.dot(members, joined, precision=lax.Precision.HIGHEST, preferred_element_type=F32)
    win[me] = jnp.concatenate([sums[:, :128], sums[:, 128:]], axis=0).astype(BF16)
    everyone(lambda p: wide(win, win_s, win_r, p).start())

    others("txt", lambda p: arrived(di_in, di_s, di_r, p))
    image_delta = jnp.sum(di_in[...].astype(F32), axis=0)
    out_img[...] = (img_ref[...].astype(F32) + iscale_ref[...].reshape(1, width) * image_delta).astype(BF16)

    everyone(lambda p: arrived(meta, meta_s, meta_r, p))
    cats = out_cat.shape[0]
    groups = [jnp.sum(meta[g * 8 : g * 8 + 8], axis=0) for g in range(n_dev // 8)]
    packed = jnp.concatenate(groups, axis=1)
    key = jnp.broadcast_to(packed % COUNT_BASE, (cats, n_dev * 16)) == iota((cats, n_dev * 16), 0)
    first = iota((cats, n_dev * 16), 1) % 16 < WINDOW
    pick_lo = jnp.logical_and(key, first)
    pick_hi = jnp.logical_and(key, jnp.logical_not(first))
    tally = jnp.sum(jnp.where(pick_lo, (packed // COUNT_BASE).astype(F32), 0.0), axis=1, keepdims=True)
    pick_lo = jnp.where(pick_lo, 1.0, 0.0).astype(BF16)
    pick_hi = jnp.where(pick_hi, 1.0, 0.0).astype(BF16)

    everyone(lambda p: arrived(win, win_s, win_r, p))
    windows = win[...].reshape(n_dev * 16, 128)
    out_cat[:, :128] = mm(pick_lo, windows) / tally
    out_cat[:, 128:] = mm(pick_hi, windows) / tally

    others("txt", lambda p: gather_copy(xi, xi_s, xi_r, "txt", p).wait_send())
    others("img", lambda p: gather_copy(xp, xp_s, xp_r, "img", p).wait_send())
    everyone(lambda p: wide(meta, meta_s, meta_r, p).wait_send())
    others("img", lambda p: gather_copy(stat_c, sc_s, sc_r, "img", p).wait_send())
    others("txt", lambda p: gather_copy(stat_r, sr_s, sr_r, "txt", p).wait_send())
    others("img", lambda p: scatter_copy(dp_out, dp_in, dp_s, dp_r, "img", p).wait_send())
    others("txt", lambda p: scatter_copy(di_out, di_in, di_s, di_r, "txt", p).wait_send())
    everyone(lambda p: wide(win, win_s, win_r, p).wait_send())


def on_device(n_img, n_txt, image_tokens, prompt_tokens, *rest):
    n_dev = n_img * n_txt
    rows, width = image_tokens.shape
    tokens = prompt_tokens.shape[0]
    embed = rest[4].shape[1]
    heads = embed // HD
    padded = (tokens + 15) // 16 * 16
    n_rows, n_cols = n_txt * rows, n_img * padded
    cats = n_dev * tokens // 16
    vmem, hbm = pl.BlockSpec(memory_space=pltpu.VMEM), pl.BlockSpec(memory_space=pl.ANY)
    dma = pltpu.SemaphoreType.DMA
    return pl.pallas_call(
        functools.partial(kernel, n_img, n_txt),
        out_shape=(
            jax.ShapeDtypeStruct((rows, width), BF16),
            jax.ShapeDtypeStruct((tokens, width), BF16),
            jax.ShapeDtypeStruct((cats, width), F32),
        ),
        in_specs=[vmem] * 6 + [hbm] * 6 + [vmem] * 2,
        out_specs=(vmem, vmem, vmem),
        scratch_shapes=[
            pltpu.VMEM((width, embed), BF16),
            pltpu.VMEM((width, embed), BF16),
            pltpu.VMEM((width, embed), BF16),
            pltpu.VMEM((width, embed), BF16),
            pltpu.VMEM((embed, width), BF16),
            pltpu.VMEM((embed, width), BF16),
            pltpu.VMEM((n_txt, rows, width), BF16),
            pltpu.VMEM((n_img, padded, width), BF16),
            pltpu.VMEM((n_dev, 1, 128), jnp.int32),
            pltpu.VMEM((heads, n_rows, HD), F32),
            pltpu.VMEM((heads, n_cols, HD), F32),
            pltpu.VMEM((n_txt, 2 * heads, n_rows), F32),
            pltpu.VMEM((n_img, 2 * heads, n_cols), F32),
            pltpu.VMEM((n_txt, rows, width), BF16),
            pltpu.VMEM((n_txt, rows, width), BF16),
            pltpu.VMEM((n_img, padded, width), BF16),
            pltpu.VMEM((n_img, padded, width), BF16),
            pltpu.VMEM((n_dev, 16, 128), BF16),
            dma((6,)),
            dma((n_txt,)), dma((n_txt,)),
            dma((n_img,)), dma((n_img,)),
            dma((n_dev,)), dma((n_dev,)),
            dma((n_txt,)), dma((n_txt,)),
            dma((n_img,)), dma((n_img,)),
            dma((n_txt,)), dma((n_txt,)),
            dma((n_img,)), dma((n_img,)),
            dma((n_dev,)), dma((n_dev,)),
        ],
        compiler_params=pltpu.CompilerParams(
            collective_id=0, has_side_effects=True, vmem_limit_bytes=56 * 2**20
        ),
        name="joining_layer",
    )(image_tokens, prompt_tokens, *rest)


def solution(mesh):
    return jax.shard_map(
        functools.partial(on_device, mesh.shape["img"], mesh.shape["txt"]),
        mesh=mesh,
        in_specs=(
            P(("img", "txt"), None),
            P(("txt", "img"), None),
            P(("txt", "img")),
            P(("txt", "img")),
        )
        + (P(),) * 10,
        out_specs=(P(("img", "txt"), None), P(("txt", "img"), None), P()),
        check_vma=False,
    )
```

time: 238 us -> 37.2 us (0.16)
  blocking collectives: 149 us -> 0 us
  waiting for transfers between devices: 50.8 us -> 0 us
  Pallas kernels: 0 us -> 33.6 us
  between operations: 15 us -> 0.66 us
  matrix products: 9.92 us -> 0 us
  other arithmetic: 9.08 us -> 0 us
    psum x3 -> x0, blocking collectives: 66.2 us -> none  [the longest x1 40.6 us: on_device(): lax.psum((category_sum, category_tally), ('img', 'txt'))]
    reduce_scatter x2 -> x0, waiting for transfers between devices: 50.8 us -> none  [the longest x1 50.8 us: on_device(): lax.psum_scatter(jnp.dot(block_rows, prompt_out_weight, preferred_element...]
    all_gather x2 -> x0, blocking collectives: 38.1 us -> none  [the longest x1 30.9 us: on_device(): lax.all_gather(prompt_normed, 'img', axis=0, tiled=True)]
    pallas_call x0 -> x1, Pallas kernels: none -> 33.6 us  [on_device(): pl.pallas_call(functools.partial(kernel, n_img, n_txt), out_shape=(jax.Sh...]
    pmax x2 -> x0, blocking collectives: 23.7 us -> none  [the longest x1 17.2 us: on_device(): col_top = lax.pmax(jnp.max(scores, axis=1), 'img')]
    unnamed x1 -> x0, blocking collectives: 21.3 us -> none
    dot_general x8 -> x0, matrix products: 9.92 us -> none  [the longest x1 2.54 us: on_device(): jnp.einsum('ihd,thd->hit', query_heads, key_heads, preferred_element_type...]
    reduce_sum x6 -> x0, other arithmetic: 4.47 us -> none  [the longest x1 2.07 us: on_device(): col_sum = lax.psum(jnp.sum(col_exp, axis=1), 'img')]
  transfers between devices with their start and end apart: 2 -> 0, of which waited for: 1 -> 0; matrix products, arithmetic and copies ran while one was open for 2% -> 0% of each run, Pallas kernels for 0% -> 0%
where the time goes in v1:
time: 37.2 us; the launch traced here: 37 us
  Pallas kernels  33.6 us (90%)
  local copies, waits for them, and re-layouts  2.72 us (7%)
  between operations  0.66 us (2%)
    pallas_call x1, Pallas kernels, on_device(): pl.pallas_call(functools.partial(kernel, n_img, n_txt), out_shape=(jax.Sh...  33.6 us
    unnamed x7, local copies, waits for them, and re-layouts  2.72 us

profile of v1, /device:TPU:0, one launch (start us, length us, event | category | flops | bytes accessed | tf_op | source)
XLA Modules:
  0.0 37.0 jit_solution(5974454897667051516)
XLA Ops:
  0.6 33.6 %joining_layer.1 = (bf16[128,256]{1,0:T(8,128)(2,1)}, bf16[24,256]{1,0:T(8,128)(2,1)}, f32[48,256]{1,0:T(8,128)}) custom-call(bf16[128,256]{1,0:T(8,128)(2,1)} %img_ref.1, bf16[24,256]{1,0:T(8,128)(2,1)} %prompt_ref.1, s32[24]{0:T(128)} %ids_ref.1, s32[24]{0:T(128)} %valid_ref.1, f32[256]{0:T(256)} %igain_ref.1, f32[256]{0:T(256)} %pgain_ref.1, ...), custom_call_target="tpu_custom_call" | custom-call | tf_op jit(solution)/shard_map/joining_layer/pallas_call | solution.py:262
  34.2 0.0 copy-start.1
  34.3 0.0 copy-start
  34.3 1.5 %copy.20 = bf16[128,256]{1,0:T(8,128)(2,1)} copy(bf16[128,256]{1,0:T(8,128)(2,1)} %get-tuple-element.6) | data formatting | bytes 131072
  35.8 0.0 copy-done.1
  35.8 0.6 %copy.21 = bf16[24,256]{1,0:T(8,128)(2,1)} copy(bf16[24,256]{1,0:T(8,128)(2,1)S(1)} %copy-done.1) | data formatting | bytes 24576
  36.4 0.0 copy-done
  36.4 0.6 %copy.22 = f32[48,256]{1,0:T(8,128)} copy(f32[48,256]{1,0:T(8,128)S(1)} %copy-done) | data formatting | bytes 98304
Async XLA Ops:
  34.2 1.5 %copy-start.1 = (bf16[24,256]{1,0:T(8,128)(2,1)S(1)}, bf16[24,256]{1,0:T(8,128)(2,1)}, u32[]{:S(2)}) copy-start(bf16[24,256]{1,0:T(8,128)(2,1)} %get-tuple-element.7) | copy-start | bytes 36868
  34.3 2.1 %copy-start = (f32[48,256]{1,0:T(8,128)S(1)}, f32[48,256]{1,0:T(8,128)}, u32[]{:S(2)}) copy-start(f32[48,256]{1,0:T(8,128)} %get-tuple-element.8) | copy-start | bytes 147460

commit v2 on v1

v2 whole, which is shorter than its diff:
```python
import functools

import jax
import jax.numpy as jnp
from jax import lax
from jax.experimental import pallas as pl
from jax.experimental.pallas import tpu as pltpu
from jax.sharding import PartitionSpec as P

HD = 256
EPSILON = 1e-05
MASKED = -1e30
FLOOR = -1e29
WINDOW = 8
COUNT_BASE = 4096
MESH = pl.DeviceIdType.MESH
F32 = jnp.float32
BF16 = jnp.bfloat16


def normalize(tokens_in, gain_row):
    values = tokens_in.astype(F32)
    average = jnp.mean(values, axis=-1, keepdims=True)
    centered = values - average
    variance = jnp.mean(centered * centered, axis=-1, keepdims=True)
    return centered * lax.rsqrt(variance + EPSILON) * gain_row


def iota(shape, dim):
    return lax.broadcasted_iota(jnp.int32, shape, dim)


def mm(a, b):
    return jnp.dot(a, b, preferred_element_type=F32)


def mm_t(a, b):
    return lax.dot_general(a, b, (((1,), (1,)), ((), ())), preferred_element_type=F32)


def kernel(
    n_img, n_txt,
    img_ref, prompt_ref, ids_ref, valid_ref, igain_ref, pgain_ref,
    wq_hbm, wk_hbm, wvi_hbm, wvp_hbm, woi_hbm, wop_hbm, iscale_ref, pscale_ref,
    out_img, out_prompt, out_cat,
    wq, wk, wvi, wvp, woi, wop, xi, xp, meta, queries, keys, values_i, values_p, exp_c, exp_r,
    stat_r, stat_c, di_out, di_in, dp_out, dp_in, win, tally, cat,
    w_sem, xi_s, xi_r, xp_s, xp_r, meta_s, meta_r, sr_s, sr_r, sc_s, sc_r,
    di_s, di_r, dp_s, dp_r, win_s, win_r, tally_s, tally_r, cat_s, cat_r,
):
    my_img, my_txt = lax.axis_index("img"), lax.axis_index("txt")
    rows, width = img_ref.shape
    half = width // 2
    tokens = prompt_ref.shape[0]
    padded = xp.shape[1]
    embed = wq.shape[1]
    heads = embed // HD
    n_rows = n_txt * rows
    n_cols = n_img * padded
    cats = out_cat.shape[0]
    cat_lanes = tally.shape[2]

    weights = ((wq_hbm, wq), (wvi_hbm, wvi), (wk_hbm, wk), (wvp_hbm, wvp), (wop_hbm, wop), (woi_hbm, woi))
    loads = [pltpu.make_async_copy(src, dst, w_sem.at[n]) for n, (src, dst) in enumerate(weights)]
    for load in loads:
        load.start()

    def others(axis, body):
        count, mine = (n_img, my_img) if axis == "img" else (n_txt, my_txt)
        if count <= 8:
            for step in range(1, count):
                body(lax.rem(mine + step, count))
        else:

            @pl.loop(1, count)
            def _(step):
                body(lax.rem(mine + step, count))

    def place(axis, p):
        return {"img": p, "txt": my_txt} if axis == "img" else {"img": my_img, "txt": p}

    barrier = pltpu.get_barrier_semaphore()
    for axis in ("img", "txt"):
        others(axis, lambda p: pl.semaphore_signal(barrier, inc=1, device_id=place(axis, p), device_id_type=MESH))

    def send(axis, src, dst, s, r):
        mine = my_img if axis == "img" else my_txt
        others(
            axis,
            lambda p: pltpu.make_async_remote_copy(
                src(p), dst.at[mine], s.at[0], r.at[0], device_id=place(axis, p), device_id_type=MESH
            ).start(),
        )

    def whole(buf, s, r):
        part = buf.at[pl.ds(0, buf.shape[0] - 1)]
        return pltpu.make_async_remote_copy(
            part, part, s.at[0], r.at[0], device_id={"img": my_img, "txt": my_txt}, device_id_type=MESH
        )

    normed = normalize(prompt_ref[...], pgain_ref[...].reshape(1, width))
    valid_row = valid_ref[...].reshape(1, tokens)
    ids_row = ids_ref[...].reshape(1, tokens)
    diagonal = iota((tokens, tokens), 0) == iota((tokens, tokens), 1)
    valid_col = jnp.sum(jnp.where(diagonal, jnp.broadcast_to(valid_row, (tokens, tokens)).astype(F32), 0.0), axis=1, keepdims=True)
    spot_start = my_img * padded
    spot = spot_start % width + iota((tokens, width), 0) == iota((tokens, width), 1)
    mark_row = jnp.sum(jnp.where(spot, valid_col, 0.0), axis=0, keepdims=True)
    spare = padded - tokens
    marks = jnp.where(iota((spare, width), 0) == spot_start // width, mark_row, 0.0)
    xp[my_img] = jnp.concatenate([normed, marks], axis=0).astype(BF16)

    first_id = ids_row[:, 0:1]
    members = jnp.logical_and(ids_row - first_id == iota((WINDOW, tokens), 0), valid_row > 0).astype(F32)
    counts = jnp.sum(members, axis=1, keepdims=True).astype(jnp.int32)
    lane = iota((WINDOW, 128), 1) - (my_img % 8) * 16
    slot = iota((WINDOW, 128), 0)
    own_lane = jnp.logical_and(jnp.logical_and(lane >= 0, lane < 16), lane % WINDOW == slot)
    meta[my_img] = jnp.sum(jnp.where(own_lane, counts * COUNT_BASE + first_id + slot, 0), axis=0, keepdims=True)

    xi[my_txt] = normalize(img_ref[...], igain_ref[...].reshape(1, width)).astype(BF16)

    pl.semaphore_wait(barrier, n_img - 1 + n_txt - 1)

    def image_copy(p, at):
        return pltpu.make_async_remote_copy(
            xi.at[at], xi.at[at], xi_s.at[p], xi_r.at[at], device_id=place("txt", p), device_id_type=MESH
        )

    others("txt", lambda p: image_copy(p, my_txt).start())
    send("img", lambda p: xp.at[my_img], xp, xp_s, xp_r)
    send("img", lambda p: meta.at[my_img], meta, meta_s, meta_r)

    def project_image(p):
        at = pl.ds(pl.multiple_of(p * rows, rows), rows)
        queries[at, :] = (mm(xi[p], wq[...]) * (HD ** -0.5)).astype(BF16)
        values_i[at, :] = mm(xi[p], wvi[...]).astype(BF16)

    loads[0].wait()
    loads[1].wait()
    project_image(my_txt)
    loads[2].wait()
    loads[3].wait()
    whole(xp, xp_s, xp_r).wait_recv()
    x_prompt = xp[...].reshape(n_cols, width)
    keys[...] = mm(x_prompt, wk[...]).astype(BF16)
    values_p[...] = mm(x_prompt, wvp[...]).astype(BF16)
    mark_rows = jnp.sum(xp[:, tokens:, :].astype(F32), axis=0)
    mask = jnp.concatenate([mark_rows[n : n + 1] for n in range(max(1, n_cols // width))], axis=1)[:, :n_cols] > 0.0

    def take_image(p):
        image_copy(p, p).wait_recv()
        project_image(p)

    others("txt", take_image)

    def over_heads(body, stats):
        if n_cols <= 512:
            for h in range(heads):
                stats = body(h, stats)
            return stats
        return lax.fori_loop(0, heads, body, stats)

    def head(h):
        return pl.ds(h * HD, HD) if isinstance(h, int) else pl.ds(pl.multiple_of(h * HD, HD), HD)

    def put(h, stats, top, total):
        at = iota(stats.shape, 1)
        return jnp.where(at == h, top, jnp.where(at == heads + h, total, stats))

    def column_head(h, stats):
        scores = mm_t(keys[:, head(h)], queries[:, head(h)])
        top = jnp.max(scores, axis=1, keepdims=True)
        exps = jnp.exp(scores - top)
        exp_c[h] = exps.astype(BF16)
        return put(h, stats, top, jnp.sum(exps, axis=1, keepdims=True))

    def row_head(h, stats):
        scores = jnp.where(mask, mm_t(queries[:, head(h)], keys[:, head(h)]), MASKED)
        top = jnp.maximum(jnp.max(scores, axis=1, keepdims=True), FLOOR)
        exps = jnp.exp(scores - top)
        exp_r[h] = exps.astype(BF16)
        return put(h, stats, top, jnp.sum(exps, axis=1, keepdims=True))

    stats = over_heads(column_head, jnp.zeros((n_cols, 128), F32))
    stat_c[my_img] = stats.T[: 2 * heads]
    send("img", lambda p: stat_c.at[my_img], stat_c, sc_s, sc_r)
    stats = over_heads(row_head, jnp.zeros((n_rows, 128), F32))
    stat_r[my_txt] = stats.T[: 2 * heads]
    send("txt", lambda p: stat_r.at[my_txt], stat_r, sr_s, sr_r)

    def factor(buf, mine):
        tops, sums = buf[:, :heads, :], buf[:, heads:, :]
        top = jnp.max(tops, axis=0)
        total = jnp.sum(sums * jnp.exp(tops - top[None]), axis=0)
        own = jnp.exp(buf[mine][:heads] - top) / total
        return jnp.concatenate([own, jnp.zeros((128 - heads, own.shape[1]), F32)], axis=0).T

    def update(exps, values, scale_of, out_weight):
        numers = [mm(exps[h], values[:, head(h)]) for h in range(heads)]
        scale = scale_of()
        delta = 0.0
        for h in range(heads):
            delta += mm((numers[h] * scale[:, h : h + 1]).astype(BF16), out_weight[head(h), :])
        return delta.astype(BF16)

    def prompt_scale():
        loads[4].wait()
        whole(stat_c, sc_s, sc_r).wait_recv()
        return factor(stat_c, my_img)

    dp_out[...] = update(exp_c, values_i, prompt_scale, wop).reshape(dp_out.shape)
    dp_in[my_img] = dp_out[my_img]
    send("img", lambda p: dp_out.at[p], dp_in, dp_s, dp_r)

    whole(meta, meta_s, meta_r).wait_recv()
    packed = jnp.concatenate([jnp.sum(meta[g * 8 : g * 8 + 8], axis=0) for g in range(n_img // 8)], axis=1)
    key = jnp.broadcast_to(packed % COUNT_BASE, (cat_lanes, n_img * 16)) == iota((cat_lanes, n_img * 16), 0)
    low = iota((cat_lanes, n_img * 16), 1) % 16 < WINDOW
    pick_lo = jnp.where(jnp.logical_and(key, low), 1.0, 0.0).astype(BF16)
    pick_hi = jnp.where(jnp.logical_and(key, jnp.logical_not(low)), 1.0, 0.0).astype(BF16)
    numbers = jnp.broadcast_to((packed // COUNT_BASE).astype(F32), (8, n_img * 16)).astype(BF16)
    tally[my_txt] = mm_t(numbers, pick_lo)
    send("txt", lambda p: tally.at[my_txt], tally, tally_s, tally_r)

    def image_scale():
        loads[5].wait()
        whole(stat_r, sr_s, sr_r).wait_recv()
        return factor(stat_r, my_txt)

    di_out[...] = update(exp_r, values_p, image_scale, woi).reshape(di_out.shape)
    di_in[my_txt] = di_out[my_txt]
    send("txt", lambda p: di_out.at[p], di_in, di_s, di_r)

    whole(dp_in, dp_s, dp_r).wait_recv()
    prompt_delta = jnp.sum(dp_in[...].astype(F32), axis=0)[:tokens]
    joined = prompt_ref[...].astype(F32) + pscale_ref[...].reshape(1, width) * prompt_delta
    sums = jnp.dot(members, joined, precision=lax.Precision.HIGHEST, preferred_element_type=F32)
    win[my_img] = jnp.concatenate([sums[:, :half], sums[:, half:]], axis=0).astype(BF16)
    send("img", lambda p: win.at[my_img], win, win_s, win_r)
    out_prompt[...] = joined.astype(BF16)

    whole(di_in, di_s, di_r).wait_recv()
    image_delta = jnp.sum(di_in[...].astype(F32), axis=0)
    out_img[...] = (img_ref[...].astype(F32) + iscale_ref[...].reshape(1, width) * image_delta).astype(BF16)

    whole(win, win_s, win_r).wait_recv()
    windows = win[...].reshape(n_img * 16, half)
    block = jnp.concatenate([mm(pick_lo[:cats], windows), mm(pick_hi[:cats], windows)], axis=1)
    cat[my_txt] = block.astype(BF16)
    send("txt", lambda p: cat.at[my_txt], cat, cat_s, cat_r)

    whole(tally, tally_s, tally_r).wait_recv()
    tally_row = jnp.sum(tally[...], axis=0)[0:1]
    on_diagonal = iota((cats, cat_lanes), 0) == iota((cats, cat_lanes), 1)
    tally_col = jnp.sum(jnp.where(on_diagonal, tally_row, 0.0), axis=1, keepdims=True)
    whole(cat, cat_s, cat_r).wait_recv()
    out_cat[...] = jnp.sum(cat[...].astype(F32), axis=0) / tally_col

    others("txt", lambda p: image_copy(p, my_txt).wait_send())
    for buf, s, r in (
        (xp, xp_s, xp_r), (meta, meta_s, meta_r), (stat_c, sc_s, sc_r), (stat_r, sr_s, sr_r), (dp_in, dp_s, dp_r),
        (tally, tally_s, tally_r), (di_in, di_s, di_r), (win, win_s, win_r), (cat, cat_s, cat_r),
    ):
        whole(buf, s, r).wait_send()


def keep(*refs):
    count = len(refs) // 2
    sems = refs[-1]
    copies = [pltpu.make_async_copy(refs[n], refs[count + n], sems.at[n]) for n in range(count)]
    for copy in copies:
        copy.start()
    for copy in copies:
        copy.wait()


def on_device(n_img, n_txt, image_tokens, prompt_tokens, *rest):
    rows, width = image_tokens.shape
    tokens = prompt_tokens.shape[0]
    embed = rest[4].shape[1]
    heads = embed // HD
    padded = (tokens + 15) // 16 * 16
    n_rows, n_cols = n_txt * rows, n_img * padded
    cats = n_img * n_txt * tokens // 16
    cat_lanes = (cats + 127) // 128 * 128
    vmem, hbm = pl.BlockSpec(memory_space=pltpu.VMEM), pl.BlockSpec(memory_space=pl.ANY)
    dma = pltpu.SemaphoreType.DMA
    one = (dma((1,)), dma((1,)))
    outs = (
        jax.ShapeDtypeStruct((rows, width), BF16),
        jax.ShapeDtypeStruct((tokens, width), BF16),
        jax.ShapeDtypeStruct((cats, width), F32),
    )
    results = pl.pallas_call(
        functools.partial(kernel, n_img, n_txt),
        out_shape=outs,
        in_specs=[vmem] * 6 + [hbm] * 6 + [vmem] * 2,
        out_specs=(vmem, vmem, vmem),
        scratch_shapes=[pltpu.VMEM((width, embed), BF16)] * 4
        + [pltpu.VMEM((embed, width), BF16)] * 2
        + [
            pltpu.VMEM((n_txt, rows, width), BF16),
            pltpu.VMEM((n_img, padded, width), BF16),
            pltpu.VMEM((n_img, 1, 128), jnp.int32),
            pltpu.VMEM((n_rows, embed), BF16),
            pltpu.VMEM((n_cols, embed), BF16),
            pltpu.VMEM((n_rows, embed), BF16),
            pltpu.VMEM((n_cols, embed), BF16),
            pltpu.VMEM((heads, n_cols, n_rows), BF16),
            pltpu.VMEM((heads, n_rows, n_cols), BF16),
            pltpu.VMEM((n_txt, 2 * heads, n_rows), F32),
            pltpu.VMEM((n_img, 2 * heads, n_cols), F32),
            pltpu.VMEM((n_txt, rows, width), BF16),
            pltpu.VMEM((n_txt, rows, width), BF16),
            pltpu.VMEM((n_img, padded, width), BF16),
            pltpu.VMEM((n_img, padded, width), BF16),
            pltpu.VMEM((n_img, 16, width // 2), BF16),
            pltpu.VMEM((n_txt, 8, cat_lanes), F32),
            pltpu.VMEM((n_txt, cats, width), BF16),
            dma((6,)),
            dma((n_txt,)),
            dma((n_txt,)),
            *one, *one, *one, *one, *one, *one, *one, *one, *one,
        ],
        compiler_params=pltpu.CompilerParams(
            collective_id=0, has_side_effects=True, vmem_limit_bytes=56 * 2**20
        ),
        name="joining_layer",
    )(image_tokens, prompt_tokens, *rest)
    return pl.pallas_call(
        keep,
        out_shape=outs,
        in_specs=[hbm] * len(outs),
        out_specs=(hbm,) * len(outs),
        scratch_shapes=[dma((len(outs),))],
        name="keep",
    )(*results)


def solution(mesh):
    return jax.shard_map(
        functools.partial(on_device, mesh.shape["img"], mesh.shape["txt"]),
        mesh=mesh,
        in_specs=(
            P(("img", "txt"), None),
            P(("txt", "img"), None),
            P(("txt", "img")),
            P(("txt", "img")),
        )
        + (P(),) * 10,
        out_specs=(P(("img", "txt"), None), P(("txt", "img"), None), P()),
        check_vma=False,
    )
```

time: 37.2 us -> 38.3 us (1.030)
  Pallas kernels: 33.6 us -> 37.5 us
  local copies, waits for them, and re-layouts: 2.72 us -> 0 us
    pallas_call x1 -> x2, Pallas kernels: 33.6 us -> 37.5 us  [the longest x1 32.5 us: on_device(): pl.pallas_call(functools.partial(kernel, n_img, n_txt), out_shape=outs, i...]
    unnamed x7 -> x0, local copies, waits for them, and re-layouts: 2.72 us -> none
where the time goes in v2:
time: 38.3 us; the launch traced here: 38.2 us
  Pallas kernels  37.5 us (98%)
  between operations  0.64 us (2%)
    pallas_call x1, Pallas kernels, on_device(): pl.pallas_call(functools.partial(kernel, n_img, n_txt), out_shape=outs, i...  32.5 us
    pallas_call x1, Pallas kernels, on_device(): pl.pallas_call(keep, out_shape=outs, in_specs=[hbm] * len(outs), out_spec...  4.98 us

profile of v2, /device:TPU:0, one launch (start us, length us, event | category | flops | bytes accessed | tf_op | source)
XLA Modules:
  0.0 38.2 jit_solution(38229504071539730)
XLA Ops:
  0.6 32.5 %joining_layer.1 = (bf16[128,256]{1,0:T(8,128)(2,1)}, bf16[24,256]{1,0:T(8,128)(2,1)}, f32[48,256]{1,0:T(8,128)}) custom-call(bf16[128,256]{1,0:T(8,128)(2,1)} %img_ref.1, bf16[24,256]{1,0:T(8,128)(2,1)} %prompt_ref.1, s32[24]{0:T(128)} %ids_ref.1, s32[24]{0:T(128)} %valid_ref.1, f32[256]{0:T(256)} %igain_ref.1, f32[256]{0:T(256)} %pgain_ref.1, ...), custom_call_target="tpu_custom_call" | custom-call | tf_op jit(solution)/shard_map/joining_layer/pallas_call | solution.py:295
  33.2 5.0 %keep.1 = (bf16[128,256]{1,0:T(8,128)(2,1)}, bf16[24,256]{1,0:T(8,128)(2,1)}, f32[48,256]{1,0:T(8,128)}) custom-call(bf16[128,256]{1,0:T(8,128)(2,1)} %get-tuple-element.6.refs_0_, bf16[24,256]{1,0:T(8,128)(2,1)} %get-tuple-element.7.refs_1_, f32[48,256]{1,0:T(8,128)} %get-tuple-element.8.refs_2_), custom_call_target="tpu_custom_call" | custom-call | tf_op jit(solution)/shard_map/keep/pallas_call | solution.py:331

commit v3 on v2

--- a/solution.py
+++ b/solution.py
@@ -13,6 +13,7 @@
 FLOOR = -1e29
 WINDOW = 8
 COUNT_BASE = 4096
+TILE = 16
 MESH = pl.DeviceIdType.MESH
 F32 = jnp.float32
 BF16 = jnp.bfloat16
@@ -30,6 +31,12 @@
     return lax.broadcasted_iota(jnp.int32, shape, dim)
 
 
+def fold(block):
+    extra = block[TILE:]
+    half = block.shape[1] // 2
+    return jnp.concatenate([block[:TILE], jnp.concatenate([extra[:, :half], extra[:, half:]], axis=0)], axis=1)
+
+
 def mm(a, b):
     return jnp.dot(a, b, preferred_element_type=F32)
 
@@ -40,30 +47,36 @@
 
 def kernel(
     n_img, n_txt,
-    img_ref, prompt_ref, ids_ref, valid_ref, igain_ref, pgain_ref,
-    wq_hbm, wk_hbm, wvi_hbm, wvp_hbm, woi_hbm, wop_hbm, iscale_ref, pscale_ref,
+    img_hbm, prompt_hbm, ids_hbm, valid_hbm, igain_hbm, pgain_hbm,
+    wq_hbm, wk_hbm, wvi_hbm, wvp_hbm, woi_hbm, wop_hbm, iscale_hbm, pscale_hbm,
     out_img, out_prompt, out_cat,
+    img_ref, prompt_ref, ids_ref, valid_ref, igain_ref, pgain_ref, iscale_ref, pscale_ref,
     wq, wk, wvi, wvp, woi, wop, xi, xp, meta, queries, keys, values_i, values_p, exp_c, exp_r,
     stat_r, stat_c, di_out, di_in, dp_out, dp_in, win, tally, cat,
-    w_sem, xi_s, xi_r, xp_s, xp_r, meta_s, meta_r, sr_s, sr_r, sc_s, sc_r,
+    in_sem, w_sem, xi_s, xi_r, relay_s, xp_s, xp_r, meta_s, meta_r, sr_s, sr_r, sc_s, sc_r,
     di_s, di_r, dp_s, dp_r, win_s, win_r, tally_s, tally_r, cat_s, cat_r,
 ):
     my_img, my_txt = lax.axis_index("img"), lax.axis_index("txt")
     rows, width = img_ref.shape
     half = width // 2
     tokens = prompt_ref.shape[0]
-    padded = xp.shape[1]
+    spare = tokens - TILE
     embed = wq.shape[1]
     heads = embed // HD
     n_rows = n_txt * rows
-    n_cols = n_img * padded
+    n_cols = n_img * tokens
     cats = out_cat.shape[0]
     cat_lanes = tally.shape[2]
 
+    inputs = (
+        (prompt_hbm, prompt_ref), (pgain_hbm, pgain_ref), (valid_hbm, valid_ref), (ids_hbm, ids_ref),
+        (img_hbm, img_ref), (igain_hbm, igain_ref), (iscale_hbm, iscale_ref), (pscale_hbm, pscale_ref),
+    )
+    fetches = [pltpu.make_async_copy(src, dst, in_sem.at[n]) for n, (src, dst) in enumerate(inputs)]
     weights = ((wq_hbm, wq), (wvi_hbm, wvi), (wk_hbm, wk), (wvp_hbm, wvp), (wop_hbm, wop), (woi_hbm, woi))
     loads = [pltpu.make_async_copy(src, dst, w_sem.at[n]) for n, (src, dst) in enumerate(weights)]
-    for load in loads:
-        load.start()
+    for fetch in fetches:
+        fetch.start()
 
     def others(axis, body):
         count, mine = (n_img, my_img) if axis == "img" else (n_txt, my_txt)
@@ -82,6 +95,8 @@
     barrier = pltpu.get_barrier_semaphore()
     for axis in ("img", "txt"):
         others(axis, lambda p: pl.semaphore_signal(barrier, inc=1, device_id=place(axis, p), device_id_type=MESH))
+    for load in loads:
+        load.start()
 
     def send(axis, src, dst, s, r):
         mine = my_img if axis == "img" else my_txt
@@ -98,26 +113,32 @@
             part, part, s.at[0], r.at[0], device_id={"img": my_img, "txt": my_txt}, device_id_type=MESH
         )
 
-    normed = normalize(prompt_ref[...], pgain_ref[...].reshape(1, width))
+    for fetch in fetches[:4]:
+        fetch.wait()
+    xp[my_img] = fold(normalize(prompt_ref[...], pgain_ref[...].reshape(1, width))).astype(BF16)
+
     valid_row = valid_ref[...].reshape(1, tokens)
     ids_row = ids_ref[...].reshape(1, tokens)
-    diagonal = iota((tokens, tokens), 0) == iota((tokens, tokens), 1)
-    valid_col = jnp.sum(jnp.where(diagonal, jnp.broadcast_to(valid_row, (tokens, tokens)).astype(F32), 0.0), axis=1, keepdims=True)
-    spot_start = my_img * padded
-    spot = spot_start % width + iota((tokens, width), 0) == iota((tokens, width), 1)
-    mark_row = jnp.sum(jnp.where(spot, valid_col, 0.0), axis=0, keepdims=True)
-    spare = padded - tokens
-    marks = jnp.where(iota((spare, width), 0) == spot_start // width, mark_row, 0.0)
-    xp[my_img] = jnp.concatenate([normed, marks], axis=0).astype(BF16)
-
     first_id = ids_row[:, 0:1]
     members = jnp.logical_and(ids_row - first_id == iota((WINDOW, tokens), 0), valid_row > 0).astype(F32)
     counts = jnp.sum(members, axis=1, keepdims=True).astype(jnp.int32)
-    lane = iota((WINDOW, 128), 1) - (my_img % 8) * 16
+    lane = iota((WINDOW, 128), 1) - (my_img % 8) * TILE
     slot = iota((WINDOW, 128), 0)
-    own_lane = jnp.logical_and(jnp.logical_and(lane >= 0, lane < 16), lane % WINDOW == slot)
-    meta[my_img] = jnp.sum(jnp.where(own_lane, counts * COUNT_BASE + first_id + slot, 0), axis=0, keepdims=True)
-
+    own_lane = jnp.logical_and(jnp.logical_and(lane >= 0, lane < TILE), lane % WINDOW == slot)
+    numbers = jnp.sum(jnp.where(own_lane, counts * COUNT_BASE + first_id + slot, 0), axis=0, keepdims=True)
+    diagonal = iota((tokens, tokens), 0) == iota((tokens, tokens), 1)
+    valid_col = jnp.sum(jnp.where(diagonal, jnp.broadcast_to(valid_row, (tokens, tokens)), 0), axis=1, keepdims=True)
+
+    def marks(at, first, count):
+        here = at + iota((count, 128), 0) == iota((count, 128), 1)
+        return jnp.sum(jnp.where(here, valid_col[first : first + count], 0), axis=0, keepdims=True)
+
+    meta[my_img] = jnp.concatenate(
+        [numbers, marks((my_img % 8) * TILE, 0, TILE), marks((my_img % (128 // spare)) * spare, TILE, spare)], axis=1
+    )
+
+    fetches[4].wait()
+    fetches[5].wait()
     xi[my_txt] = normalize(img_ref[...], igain_ref[...].reshape(1, width)).astype(BF16)
 
     pl.semaphore_wait(barrier, n_img - 1 + n_txt - 1)
@@ -127,8 +148,12 @@
             xi.at[at], xi.at[at], xi_s.at[p], xi_r.at[at], device_id=place("txt", p), device_id_type=MESH
         )
 
-    others("txt", lambda p: image_copy(p, my_txt).start())
+    mate = my_txt + 1 - 2 * (my_txt % 2)
+    far = [lax.rem(my_txt + 2 * step, n_txt) for step in range(1, n_txt // 2)]
     send("img", lambda p: xp.at[my_img], xp, xp_s, xp_r)
+    for p in far:
+        image_copy(p, my_txt).start()
+    image_copy(mate, my_txt).start()
     send("img", lambda p: meta.at[my_img], meta, meta_s, meta_r)
 
     def project_image(p):
@@ -142,17 +167,36 @@
     loads[2].wait()
     loads[3].wait()
     whole(xp, xp_s, xp_r).wait_recv()
-    x_prompt = xp[...].reshape(n_cols, width)
+    tall = xp[:, :, :width].reshape(n_img * TILE, width)
+    short = xp[:, :, width:].astype(F32)
+    short = jnp.concatenate([short[:, :spare], short[:, spare:]], axis=2).reshape(n_img * spare, width)
+    x_prompt = jnp.concatenate([tall, short.astype(BF16)], axis=0)
     keys[...] = mm(x_prompt, wk[...]).astype(BF16)
     values_p[...] = mm(x_prompt, wvp[...]).astype(BF16)
-    mark_rows = jnp.sum(xp[:, tokens:, :].astype(F32), axis=0)
-    mask = jnp.concatenate([mark_rows[n : n + 1] for n in range(max(1, n_cols // width))], axis=1)[:, :n_cols] > 0.0
-
-    def take_image(p):
+
+    def relay(p):
+        return pltpu.make_async_remote_copy(
+            xi.at[p], xi.at[p], relay_s.at[p], xi_r.at[p], device_id=place("txt", mate), device_id_type=MESH
+        )
+
+    for p in far:
         image_copy(p, p).wait_recv()
+        relay(p).start()
+    image_copy(mate, mate).wait_recv()
+    project_image(mate)
+    for p in far:
         project_image(p)
 
-    others("txt", take_image)
+    whole(meta, meta_s, meta_r).wait_recv()
+    per = 128 // spare
+    tall_marks = [jnp.sum(meta[g * 8 : g * 8 + 8, :, 128:256], axis=0) for g in range(n_img // 8)]
+    short_marks = [jnp.sum(meta[g : min(g + per, n_img), :, 256:], axis=0) for g in range(0, n_img, per)]
+    mask = jnp.concatenate(tall_marks + short_marks, axis=1)[:, :n_cols] > 0
+
+    for p in far:
+        there = p + 1 - 2 * (p % 2)
+        image_copy(there, there).wait_recv()
+        project_image(there)
 
     def over_heads(body, stats):
         if n_cols <= 512:
@@ -202,19 +246,22 @@
         delta = 0.0
         for h in range(heads):
             delta += mm((numers[h] * scale[:, h : h + 1]).astype(BF16), out_weight[head(h), :])
-        return delta.astype(BF16)
+        return delta
 
     def prompt_scale():
         loads[4].wait()
         whole(stat_c, sc_s, sc_r).wait_recv()
         return factor(stat_c, my_img)
 
-    dp_out[...] = update(exp_c, values_i, prompt_scale, wop).reshape(dp_out.shape)
+    delta = update(exp_c, values_i, prompt_scale, wop)
+    tall = delta[: n_img * TILE].reshape(n_img, TILE, width)
+    short = delta[n_img * TILE :].reshape(n_img, spare, width)
+    short = jnp.concatenate([short[:, :, :half], short[:, :, half:]], axis=1)
+    dp_out[...] = jnp.concatenate([tall, short], axis=2).astype(BF16)
     dp_in[my_img] = dp_out[my_img]
     send("img", lambda p: dp_out.at[p], dp_in, dp_s, dp_r)
 
-    whole(meta, meta_s, meta_r).wait_recv()
-    packed = jnp.concatenate([jnp.sum(meta[g * 8 : g * 8 + 8], axis=0) for g in range(n_img // 8)], axis=1)
+    packed = jnp.concatenate([jnp.sum(meta[g * 8 : g * 8 + 8, :, :128], axis=0) for g in range(n_img // 8)], axis=1)
     key = jnp.broadcast_to(packed % COUNT_BASE, (cat_lanes, n_img * 16)) == iota((cat_lanes, n_img * 16), 0)
     low = iota((cat_lanes, n_img * 16), 1) % 16 < WINDOW
     pick_lo = jnp.where(jnp.logical_and(key, low), 1.0, 0.0).astype(BF16)
@@ -228,12 +275,16 @@
         whole(stat_r, sr_s, sr_r).wait_recv()
         return factor(stat_r, my_txt)
 
-    di_out[...] = update(exp_r, values_p, image_scale, woi).reshape(di_out.shape)
+    di_out[...] = update(exp_r, values_p, image_scale, woi).astype(BF16).reshape(di_out.shape)
     di_in[my_txt] = di_out[my_txt]
     send("txt", lambda p: di_out.at[p], di_in, di_s, di_r)
 
     whole(dp_in, dp_s, dp_r).wait_recv()
-    prompt_delta = jnp.sum(dp_in[...].astype(F32), axis=0)[:tokens]
+    total = jnp.sum(dp_in[...].astype(F32), axis=0)
+    short = jnp.concatenate([total[:spare, width:], total[spare:, width:]], axis=1)
+    prompt_delta = jnp.concatenate([total[:, :width], short], axis=0)
+    fetches[6].wait()
+    fetches[7].wait()
     joined = prompt_ref[...].astype(F32) + pscale_ref[...].reshape(1, width) * prompt_delta
     sums = jnp.dot(members, joined, precision=lax.Precision.HIGHEST, preferred_element_type=F32)
     win[my_img] = jnp.concatenate([sums[:, :half], sums[:, half:]], axis=0).astype(BF16)
@@ -257,7 +308,10 @@
     whole(cat, cat_s, cat_r).wait_recv()
     out_cat[...] = jnp.sum(cat[...].astype(F32), axis=0) / tally_col
 
-    others("txt", lambda p: image_copy(p, my_txt).wait_send())
+    for p in far:
+        image_copy(p, my_txt).wait_send()
+        relay(p).wait_send()
+    image_copy(mate, my_txt).wait_send()
     for buf, s, r in (
         (xp, xp_s, xp_r), (meta, meta_s, meta_r), (stat_c, sc_s, sc_r), (stat_r, sr_s, sr_r), (dp_in, dp_s, dp_r),
         (tally, tally_s, tally_r), (di_in, di_s, di_r), (win, win_s, win_r), (cat, cat_s, cat_r),
@@ -267,12 +321,8 @@
 
 def keep(*refs):
     count = len(refs) // 2
-    sems = refs[-1]
-    copies = [pltpu.make_async_copy(refs[n], refs[count + n], sems.at[n]) for n in range(count)]
-    for copy in copies:
-        copy.start()
-    for copy in copies:
-        copy.wait()
+    for n in range(count):
+        refs[count + n][...] = refs[n][...]
 
 
 def on_device(n_img, n_txt, image_tokens, prompt_tokens, *rest):
@@ -280,8 +330,8 @@
     tokens = prompt_tokens.shape[0]
     embed = rest[4].shape[1]
     heads = embed // HD
-    padded = (tokens + 15) // 16 * 16
-    n_rows, n_cols = n_txt * rows, n_img * padded
+    n_rows, n_cols = n_txt * rows, n_img * tokens
+    folded = width + width // 2
     cats = n_img * n_txt * tokens // 16
     cat_lanes = (cats + 127) // 128 * 128
     vmem, hbm = pl.BlockSpec(memory_space=pltpu.VMEM), pl.BlockSpec(memory_space=pl.ANY)
@@ -294,15 +344,16 @@
     )
     results = pl.pallas_call(
         functools.partial(kernel, n_img, n_txt),
-        out_shape=outs,
-        in_specs=[vmem] * 6 + [hbm] * 6 + [vmem] * 2,
+        out_shape=tuple(pltpu.VMEM(out.shape, out.dtype) for out in outs),
+        in_specs=[hbm] * 14,
         out_specs=(vmem, vmem, vmem),
-        scratch_shapes=[pltpu.VMEM((width, embed), BF16)] * 4
+        scratch_shapes=[pltpu.VMEM(x.shape, x.dtype) for x in (image_tokens, prompt_tokens, *rest[:4], *rest[10:])]
+        + [pltpu.VMEM((width, embed), BF16)] * 4
         + [pltpu.VMEM((embed, width), BF16)] * 2
         + [
             pltpu.VMEM((n_txt, rows, width), BF16),
-            pltpu.VMEM((n_img, padded, width), BF16),
-            pltpu.VMEM((n_img, 1, 128), jnp.int32),
+            pltpu.VMEM((n_img, TILE, folded), BF16),
+            pltpu.VMEM((n_img, 1, 384), jnp.int32),
             pltpu.VMEM((n_rows, embed), BF16),
             pltpu.VMEM((n_cols, embed), BF16),
             pltpu.VMEM((n_rows, embed), BF16),
@@ -313,12 +364,14 @@
             pltpu.VMEM((n_img, 2 * heads, n_cols), F32),
             pltpu.VMEM((n_txt, rows, width), BF16),
             pltpu.VMEM((n_txt, rows, width), BF16),
-            pltpu.VMEM((n_img, padded, width), BF16),
-            pltpu.VMEM((n_img, padded, width), BF16),
+            pltpu.VMEM((n_img, TILE, folded), BF16),
+            pltpu.VMEM((n_img, TILE, folded), BF16),
             pltpu.VMEM((n_img, 16, width // 2), BF16),
             pltpu.VMEM((n_txt, 8, cat_lanes), F32),
             pltpu.VMEM((n_txt, cats, width), BF16),
+            dma((8,)),
             dma((6,)),
+            dma((n_txt,)),
             dma((n_txt,)),
             dma((n_txt,)),
             *one, *one, *one, *one, *one, *one, *one, *one, *one,
@@ -331,9 +384,9 @@
     return pl.pallas_call(
         keep,
         out_shape=outs,
-        in_specs=[hbm] * len(outs),
-        out_specs=(hbm,) * len(outs),
-        scratch_shapes=[dma((len(outs),))],
+        in_specs=[vmem] * len(outs),
+        out_specs=(vmem,) * len(outs),
+        compiler_params=pltpu.CompilerParams(vmem_limit_bytes=2**20),
         name="keep",
     )(*results)
 

time: 38.3 us -> 31.6 us (0.83)
  Pallas kernels: 37.5 us -> 30.7 us
    pallas_call x2, Pallas kernels: 37.5 us -> 30.7 us  [the longest x1 30.1 us: on_device(): pl.pallas_call(functools.partial(kernel, n_img, n_txt), out_shape=tuple((...]
where the time goes in v3:
time: 31.6 us; the launch traced here: 31.4 us
  Pallas kernels  30.7 us (97%)
  between operations  0.64 us (2%)
    pallas_call x1, Pallas kernels, on_device(): pl.pallas_call(functools.partial(kernel, n_img, n_txt), out_shape=tuple((...  30.1 us
    pallas_call x1, Pallas kernels, on_device(): pl.pallas_call(keep, out_shape=outs, in_specs=[vmem] * len(outs), out_spe...  0.66 us

profile of v3, /device:TPU:0, one launch (start us, length us, event | category | flops | bytes accessed | tf_op | source)
XLA Modules:
  0.0 31.4 jit_solution(17713600925411896135)
XLA Ops:
  0.6 30.1 %joining_layer.1 = (bf16[128,256]{1,0:T(8,128)(2,1)S(1)}, bf16[24,256]{1,0:T(8,128)(2,1)S(1)}, f32[48,256]{1,0:T(8,128)S(1)}) custom-call(bf16[128,256]{1,0:T(8,128)(2,1)} %img_hbm.1, bf16[24,256]{1,0:T(8,128)(2,1)} %prompt_hbm.1, s32[24]{0:T(128)} %ids_hbm.1, s32[24]{0:T(128)} %valid_hbm.1, f32[256]{0:T(256)} %igain_hbm.1, f32[256]{0:T(256)} %pgain_hbm.1, ...), custom_call_target="tpu_custom_call" | custom-call | tf_op jit(solution)/shard_map/joining_layer/pallas_call | solution.py:345
  30.7 0.7 %keep.1 = (bf16[128,256]{1,0:T(8,128)(2,1)}, bf16[24,256]{1,0:T(8,128)(2,1)}, f32[48,256]{1,0:T(8,128)}) custom-call(bf16[128,256]{1,0:T(8,128)(2,1)S(1)} %get-tuple-element.6.refs_0_, bf16[24,256]{1,0:T(8,128)(2,1)S(1)} %get-tuple-element.7.refs_1_, f32[48,256]{1,0:T(8,128)S(1)} %get-tuple-element.8.refs_2_), custom_call_target="tpu_custom_call" | custom-call | tf_op jit(solution)/shard_map/keep/pallas_call | solution.py:384

commit v4 on v3

--- a/solution.py
+++ b/solution.py
@@ -81,7 +81,7 @@
     def others(axis, body):
         count, mine = (n_img, my_img) if axis == "img" else (n_txt, my_txt)
         if count <= 8:
-            for step in range(1, count):
+            for step in sorted(range(1, count), key=lambda n: abs(2 * n - count)):
                 body(lax.rem(mine + step, count))
         else:
 
@@ -156,47 +156,45 @@
     image_copy(mate, my_txt).start()
     send("img", lambda p: meta.at[my_img], meta, meta_s, meta_r)
 
-    def project_image(p):
-        at = pl.ds(pl.multiple_of(p * rows, rows), rows)
-        queries[at, :] = (mm(xi[p], wq[...]) * (HD ** -0.5)).astype(BF16)
-        values_i[at, :] = mm(xi[p], wvi[...]).astype(BF16)
+    def image_rows(p):
+        return pl.ds(pl.multiple_of(p * rows, rows), rows)
+
+    def project_queries(p):
+        queries[image_rows(p), :] = (mm(xi[p], wq[...]) * (HD ** -0.5)).astype(BF16)
+
+    def project_values(p):
+        values_i[image_rows(p), :] = mm(xi[p], wvi[...]).astype(BF16)
+
+    def relay(p):
+        return pltpu.make_async_remote_copy(
+            xi.at[p], xi.at[p], relay_s.at[p], xi_r.at[p], device_id=place("txt", mate), device_id_type=MESH
+        )
 
     loads[0].wait()
+    project_queries(my_txt)
+    for p in far:
+        image_copy(p, p).wait_recv()
+        relay(p).start()
     loads[1].wait()
-    project_image(my_txt)
-    loads[2].wait()
-    loads[3].wait()
+    project_values(my_txt)
+    image_copy(mate, mate).wait_recv()
+    project_queries(mate)
+    project_values(mate)
+    for p in far:
+        project_queries(p)
+        project_values(p)
+
     whole(xp, xp_s, xp_r).wait_recv()
     tall = xp[:, :, :width].reshape(n_img * TILE, width)
     short = xp[:, :, width:].astype(F32)
     short = jnp.concatenate([short[:, :spare], short[:, spare:]], axis=2).reshape(n_img * spare, width)
     x_prompt = jnp.concatenate([tall, short.astype(BF16)], axis=0)
+    loads[2].wait()
     keys[...] = mm(x_prompt, wk[...]).astype(BF16)
-    values_p[...] = mm(x_prompt, wvp[...]).astype(BF16)
-
-    def relay(p):
-        return pltpu.make_async_remote_copy(
-            xi.at[p], xi.at[p], relay_s.at[p], xi_r.at[p], device_id=place("txt", mate), device_id_type=MESH
-        )
-
-    for p in far:
+    beyond = [p + 1 - 2 * (p % 2) for p in far]
+    for p in beyond:
         image_copy(p, p).wait_recv()
-        relay(p).start()
-    image_copy(mate, mate).wait_recv()
-    project_image(mate)
-    for p in far:
-        project_image(p)
-
-    whole(meta, meta_s, meta_r).wait_recv()
-    per = 128 // spare
-    tall_marks = [jnp.sum(meta[g * 8 : g * 8 + 8, :, 128:256], axis=0) for g in range(n_img // 8)]
-    short_marks = [jnp.sum(meta[g : min(g + per, n_img), :, 256:], axis=0) for g in range(0, n_img, per)]
-    mask = jnp.concatenate(tall_marks + short_marks, axis=1)[:, :n_cols] > 0
-
-    for p in far:
-        there = p + 1 - 2 * (p % 2)
-        image_copy(there, there).wait_recv()
-        project_image(there)
+        project_queries(p)
 
     def over_heads(body, stats):
         if n_cols <= 512:
@@ -229,6 +227,15 @@
     stats = over_heads(column_head, jnp.zeros((n_cols, 128), F32))
     stat_c[my_img] = stats.T[: 2 * heads]
     send("img", lambda p: stat_c.at[my_img], stat_c, sc_s, sc_r)
+    loads[3].wait()
+    for p in beyond:
+        project_values(p)
+    values_p[...] = mm(x_prompt, wvp[...]).astype(BF16)
+    whole(meta, meta_s, meta_r).wait_recv()
+    per = 128 // spare
+    tall_marks = [jnp.sum(meta[g * 8 : g * 8 + 8, :, 128:256], axis=0) for g in range(n_img // 8)]
+    short_marks = [jnp.sum(meta[g : min(g + per, n_img), :, 256:], axis=0) for g in range(0, n_img, per)]
+    mask = jnp.concatenate(tall_marks + short_marks, axis=1)[:, :n_cols] > 0
     stats = over_heads(row_head, jnp.zeros((n_rows, 128), F32))
     stat_r[my_txt] = stats.T[: 2 * heads]
     send("txt", lambda p: stat_r.at[my_txt], stat_r, sr_s, sr_r)
@@ -240,20 +247,20 @@
         own = jnp.exp(buf[mine][:heads] - top) / total
         return jnp.concatenate([own, jnp.zeros((128 - heads, own.shape[1]), F32)], axis=0).T
 
-    def update(exps, values, scale_of, out_weight):
-        numers = [mm(exps[h], values[:, head(h)]) for h in range(heads)]
-        scale = scale_of()
+    def numerators(exps, values):
+        return [mm(exps[h], values[:, head(h)]) for h in range(heads)]
+
+    def update(numers, scale, out_weight):
         delta = 0.0
         for h in range(heads):
             delta += mm((numers[h] * scale[:, h : h + 1]).astype(BF16), out_weight[head(h), :])
         return delta
 
-    def prompt_scale():
-        loads[4].wait()
-        whole(stat_c, sc_s, sc_r).wait_recv()
-        return factor(stat_c, my_img)
-
-    delta = update(exp_c, values_i, prompt_scale, wop)
+    numers_p = numerators(exp_c, values_i)
+    numers_i = numerators(exp_r, values_p)
+    loads[4].wait()
+    whole(stat_c, sc_s, sc_r).wait_recv()
+    delta = update(numers_p, factor(stat_c, my_img), wop)
     tall = delta[: n_img * TILE].reshape(n_img, TILE, width)
     short = delta[n_img * TILE :].reshape(n_img, spare, width)
     short = jnp.concatenate([short[:, :, :half], short[:, :, half:]], axis=1)
@@ -270,12 +277,9 @@
     tally[my_txt] = mm_t(numbers, pick_lo)
     send("txt", lambda p: tally.at[my_txt], tally, tally_s, tally_r)
 
-    def image_scale():
-        loads[5].wait()
-        whole(stat_r, sr_s, sr_r).wait_recv()
-        return factor(stat_r, my_txt)
-
-    di_out[...] = update(exp_r, values_p, image_scale, woi).astype(BF16).reshape(di_out.shape)
+    loads[5].wait()
+    whole(stat_r, sr_s, sr_r).wait_recv()
+    di_out[...] = update(numers_i, factor(stat_r, my_txt), woi).astype(BF16).reshape(di_out.shape)
     di_in[my_txt] = di_out[my_txt]
     send("txt", lambda p: di_out.at[p], di_in, di_s, di_r)
 

time: 31.6 us -> 31.6 us (level)
  no operation moved by 1% of the time
where the time goes in v4:
time: 31.6 us; the launch traced here: 31.4 us
  Pallas kernels  30.7 us (97%)
  between operations  0.64 us (2%)
    pallas_call x1, Pallas kernels, on_device(): pl.pallas_call(functools.partial(kernel, n_img, n_txt), out_shape=tuple((...  30.1 us
    pallas_call x1, Pallas kernels, on_device(): pl.pallas_call(keep, out_shape=outs, in_specs=[vmem] * len(outs), out_spe...  0.66 us

profile of v4, /device:TPU:0, one launch (start us, length us, event | category | flops | bytes accessed | tf_op | source)
XLA Modules:
  0.0 31.4 jit_solution(3071532029118376197)
XLA Ops:
  0.6 30.1 %joining_layer.1 = (bf16[128,256]{1,0:T(8,128)(2,1)S(1)}, bf16[24,256]{1,0:T(8,128)(2,1)S(1)}, f32[48,256]{1,0:T(8,128)S(1)}) custom-call(bf16[128,256]{1,0:T(8,128)(2,1)} %img_hbm.1, bf16[24,256]{1,0:T(8,128)(2,1)} %prompt_hbm.1, s32[24]{0:T(128)} %ids_hbm.1, s32[24]{0:T(128)} %valid_hbm.1, f32[256]{0:T(256)} %igain_hbm.1, f32[256]{0:T(256)} %pgain_hbm.1, ...), custom_call_target="tpu_custom_call" | custom-call | tf_op jit(solution)/shard_map/joining_layer/pallas_call | solution.py:349
  30.7 0.7 %keep.1 = (bf16[128,256]{1,0:T(8,128)(2,1)}, bf16[24,256]{1,0:T(8,128)(2,1)}, f32[48,256]{1,0:T(8,128)}) custom-call(bf16[128,256]{1,0:T(8,128)(2,1)S(1)} %get-tuple-element.6.refs_0_, bf16[24,256]{1,0:T(8,128)(2,1)S(1)} %get-tuple-element.7.refs_1_, f32[48,256]{1,0:T(8,128)S(1)} %get-tuple-element.8.refs_2_), custom_call_target="tpu_custom_call" | custom-call | tf_op jit(solution)/shard_map/keep/pallas_call | solution.py:388

commit v5 on v4

--- a/solution.py
+++ b/solution.py
@@ -227,37 +227,32 @@
     stats = over_heads(column_head, jnp.zeros((n_cols, 128), F32))
     stat_c[my_img] = stats.T[: 2 * heads]
     send("img", lambda p: stat_c.at[my_img], stat_c, sc_s, sc_r)
-    loads[3].wait()
+    def factor(buf, mine):
+        tops, sums = buf[:, :heads, :], buf[:, heads:, :]
+        top = jnp.max(tops, axis=0)
+        total = jnp.sum(sums * jnp.exp(tops - top[None]), axis=0)
+        own = jnp.exp(buf[mine][:heads] - top) / total
+        return jnp.concatenate([own, jnp.zeros((128 - heads, own.shape[1]), F32)], axis=0).T
+
+    def numerators(exps, values):
+        return [mm(exps[h], values[:, head(h)]) for h in range(heads)]
+
+    def update(numers, scale, out_weight):
+        delta = 0.0
+        for h in range(heads):
+            delta += mm((numers[h] * scale[:, h : h + 1]).astype(BF16), out_weight[head(h), :])
+        return delta
+
     for p in beyond:
         project_values(p)
+    numers_p = numerators(exp_c, values_i)
+    loads[3].wait()
     values_p[...] = mm(x_prompt, wvp[...]).astype(BF16)
     whole(meta, meta_s, meta_r).wait_recv()
     per = 128 // spare
     tall_marks = [jnp.sum(meta[g * 8 : g * 8 + 8, :, 128:256], axis=0) for g in range(n_img // 8)]
     short_marks = [jnp.sum(meta[g : min(g + per, n_img), :, 256:], axis=0) for g in range(0, n_img, per)]
     mask = jnp.concatenate(tall_marks + short_marks, axis=1)[:, :n_cols] > 0
-    stats = over_heads(row_head, jnp.zeros((n_rows, 128), F32))
-    stat_r[my_txt] = stats.T[: 2 * heads]
-    send("txt", lambda p: stat_r.at[my_txt], stat_r, sr_s, sr_r)
-
-    def factor(buf, mine):
-        tops, sums = buf[:, :heads, :], buf[:, heads:, :]
-        top = jnp.max(tops, axis=0)
-        total = jnp.sum(sums * jnp.exp(tops - top[None]), axis=0)
-        own = jnp.exp(buf[mine][:heads] - top) / total
-        return jnp.concatenate([own, jnp.zeros((128 - heads, own.shape[1]), F32)], axis=0).T
-
-    def numerators(exps, values):
-        return [mm(exps[h], values[:, head(h)]) for h in range(heads)]
-
-    def update(numers, scale, out_weight):
-        delta = 0.0
-        for h in range(heads):
-            delta += mm((numers[h] * scale[:, h : h + 1]).astype(BF16), out_weight[head(h), :])
-        return delta
-
-    numers_p = numerators(exp_c, values_i)
-    numers_i = numerators(exp_r, values_p)
     loads[4].wait()
     whole(stat_c, sc_s, sc_r).wait_recv()
     delta = update(numers_p, factor(stat_c, my_img), wop)
@@ -268,6 +263,10 @@
     dp_in[my_img] = dp_out[my_img]
     send("img", lambda p: dp_out.at[p], dp_in, dp_s, dp_r)
 
+    stats = over_heads(row_head, jnp.zeros((n_rows, 128), F32))
+    stat_r[my_txt] = stats.T[: 2 * heads]
+    send("txt", lambda p: stat_r.at[my_txt], stat_r, sr_s, sr_r)
+
     packed = jnp.concatenate([jnp.sum(meta[g * 8 : g * 8 + 8, :, :128], axis=0) for g in range(n_img // 8)], axis=1)
     key = jnp.broadcast_to(packed % COUNT_BASE, (cat_lanes, n_img * 16)) == iota((cat_lanes, n_img * 16), 0)
     low = iota((cat_lanes, n_img * 16), 1) % 16 < WINDOW
@@ -277,11 +276,7 @@
     tally[my_txt] = mm_t(numbers, pick_lo)
     send("txt", lambda p: tally.at[my_txt], tally, tally_s, tally_r)
 
-    loads[5].wait()
-    whole(stat_r, sr_s, sr_r).wait_recv()
-    di_out[...] = update(numers_i, factor(stat_r, my_txt), woi).astype(BF16).reshape(di_out.shape)
-    di_in[my_txt] = di_out[my_txt]
-    send("txt", lambda p: di_out.at[p], di_in, di_s, di_r)
+    numers_i = numerators(exp_r, values_p)
 
     whole(dp_in, dp_s, dp_r).wait_recv()
     total = jnp.sum(dp_in[...].astype(F32), axis=0)
@@ -295,15 +290,21 @@
     send("img", lambda p: win.at[my_img], win, win_s, win_r)
     out_prompt[...] = joined.astype(BF16)
 
-    whole(di_in, di_s, di_r).wait_recv()
-    image_delta = jnp.sum(di_in[...].astype(F32), axis=0)
-    out_img[...] = (img_ref[...].astype(F32) + iscale_ref[...].reshape(1, width) * image_delta).astype(BF16)
+    loads[5].wait()
+    whole(stat_r, sr_s, sr_r).wait_recv()
+    di_out[...] = update(numers_i, factor(stat_r, my_txt), woi).astype(BF16).reshape(di_out.shape)
+    di_in[my_txt] = di_out[my_txt]
+    send("txt", lambda p: di_out.at[p], di_in, di_s, di_r)
 
     whole(win, win_s, win_r).wait_recv()
     windows = win[...].reshape(n_img * 16, half)
     block = jnp.concatenate([mm(pick_lo[:cats], windows), mm(pick_hi[:cats], windows)], axis=1)
     cat[my_txt] = block.astype(BF16)
     send("txt", lambda p: cat.at[my_txt], cat, cat_s, cat_r)
+
+    whole(di_in, di_s, di_r).wait_recv()
+    image_delta = jnp.sum(di_in[...].astype(F32), axis=0)
+    out_img[...] = (img_ref[...].astype(F32) + iscale_ref[...].reshape(1, width) * image_delta).astype(BF16)
 
     whole(tally, tally_s, tally_r).wait_recv()
     tally_row = jnp.sum(tally[...], axis=0)[0:1]

time: 31.6 us -> 31.6 us (level)
  no operation moved by 1% of the time
where the time goes in v5:
time: 31.6 us; the launch traced here: 31.4 us
  Pallas kernels  30.7 us (97%)
  between operations  0.64 us (2%)
    pallas_call x1, Pallas kernels, on_device(): pl.pallas_call(functools.partial(kernel, n_img, n_txt), out_shape=tuple((...  30.1 us
    pallas_call x1, Pallas kernels, on_device(): pl.pallas_call(keep, out_shape=outs, in_specs=[vmem] * len(outs), out_spe...  0.66 us

profile of v5, /device:TPU:0, one launch (start us, length us, event | category | flops | bytes accessed | tf_op | source)
XLA Modules:
  0.0 31.4 jit_solution(9034621641406444997)
XLA Ops:
  0.6 30.1 %joining_layer.1 = (bf16[128,256]{1,0:T(8,128)(2,1)S(1)}, bf16[24,256]{1,0:T(8,128)(2,1)S(1)}, f32[48,256]{1,0:T(8,128)S(1)}) custom-call(bf16[128,256]{1,0:T(8,128)(2,1)} %img_hbm.1, bf16[24,256]{1,0:T(8,128)(2,1)} %prompt_hbm.1, s32[24]{0:T(128)} %ids_hbm.1, s32[24]{0:T(128)} %valid_hbm.1, f32[256]{0:T(256)} %igain_hbm.1, f32[256]{0:T(256)} %pgain_hbm.1, ...), custom_call_target="tpu_custom_call" | custom-call | tf_op jit(solution)/shard_map/joining_layer/pallas_call | solution.py:350
  30.7 0.7 %keep.1 = (bf16[128,256]{1,0:T(8,128)(2,1)}, bf16[24,256]{1,0:T(8,128)(2,1)}, f32[48,256]{1,0:T(8,128)}) custom-call(bf16[128,256]{1,0:T(8,128)(2,1)S(1)} %get-tuple-element.6.refs_0_, bf16[24,256]{1,0:T(8,128)(2,1)S(1)} %get-tuple-element.7.refs_1_, f32[48,256]{1,0:T(8,128)S(1)} %get-tuple-element.8.refs_2_), custom_call_target="tpu_custom_call" | custom-call | tf_op jit(solution)/shard_map/keep/pallas_call | solution.py:389

commit v6 on v5

--- a/solution.py
+++ b/solution.py
@@ -51,7 +51,8 @@
     wq_hbm, wk_hbm, wvi_hbm, wvp_hbm, woi_hbm, wop_hbm, iscale_hbm, pscale_hbm,
     out_img, out_prompt, out_cat,
     img_ref, prompt_ref, ids_ref, valid_ref, igain_ref, pgain_ref, iscale_ref, pscale_ref,
-    wq, wk, wvi, wvp, woi, wop, xi, xp, meta, queries, keys, values_i, values_p, exp_c, exp_r,
+    wq, wk, wvi, wvp, woi, wop, xi, xp, meta, queries, keys, values_i, values_p, exp_c,
+    x_prompt, seen_c, seen_r, numer_p, numer_i, sum_p, sum_i,
     stat_r, stat_c, di_out, di_in, dp_out, dp_in, win, tally, cat,
     in_sem, w_sem, xi_s, xi_r, relay_s, xp_s, xp_r, meta_s, meta_r, sr_s, sr_r, sc_s, sc_r,
     di_s, di_r, dp_s, dp_r, win_s, win_r, tally_s, tally_r, cat_s, cat_r,
@@ -141,6 +142,8 @@
     fetches[5].wait()
     xi[my_txt] = normalize(img_ref[...], igain_ref[...].reshape(1, width)).astype(BF16)
 
+    seen_c[...] = jnp.zeros(seen_c.shape, F32)
+    seen_r[...] = jnp.zeros(seen_r.shape, F32)
     pl.semaphore_wait(barrier, n_img - 1 + n_txt - 1)
 
     def image_copy(p, at):
@@ -159,11 +162,18 @@
     def image_rows(p):
         return pl.ds(pl.multiple_of(p * rows, rows), rows)
 
+    def head(h):
+        return pl.ds(pl.multiple_of(h * HD, HD), HD)
+
     def project_queries(p):
-        queries[image_rows(p), :] = (mm(xi[p], wq[...]) * (HD ** -0.5)).astype(BF16)
+        @pl.loop(0, heads)
+        def _(h):
+            queries[image_rows(p), head(h)] = (mm(xi[p], wq[:, head(h)]) * (HD ** -0.5)).astype(BF16)
 
     def project_values(p):
-        values_i[image_rows(p), :] = mm(xi[p], wvi[...]).astype(BF16)
+        @pl.loop(0, heads)
+        def _(h):
+            values_i[image_rows(p), head(h)] = mm(xi[p], wvi[:, head(h)]).astype(BF16)
 
     def relay(p):
         return pltpu.make_async_remote_copy(
@@ -188,45 +198,33 @@
     tall = xp[:, :, :width].reshape(n_img * TILE, width)
     short = xp[:, :, width:].astype(F32)
     short = jnp.concatenate([short[:, :spare], short[:, spare:]], axis=2).reshape(n_img * spare, width)
-    x_prompt = jnp.concatenate([tall, short.astype(BF16)], axis=0)
+    x_prompt[...] = jnp.concatenate([tall, short.astype(BF16)], axis=0)
     loads[2].wait()
-    keys[...] = mm(x_prompt, wk[...]).astype(BF16)
+
+    @pl.loop(0, heads)
+    def _(h):
+        keys[:, head(h)] = mm(x_prompt[...], wk[:, head(h)]).astype(BF16)
+
     beyond = [p + 1 - 2 * (p % 2) for p in far]
     for p in beyond:
         image_copy(p, p).wait_recv()
         project_queries(p)
 
-    def over_heads(body, stats):
-        if n_cols <= 512:
-            for h in range(heads):
-                stats = body(h, stats)
-            return stats
-        return lax.fori_loop(0, heads, body, stats)
-
-    def head(h):
-        return pl.ds(h * HD, HD) if isinstance(h, int) else pl.ds(pl.multiple_of(h * HD, HD), HD)
-
     def put(h, stats, top, total):
         at = iota(stats.shape, 1)
-        return jnp.where(at == h, top, jnp.where(at == heads + h, total, stats))
-
-    def column_head(h, stats):
+        stats[...] = jnp.where(at == h, top, jnp.where(at == heads + h, total, stats[...]))
+
+    @pl.loop(0, heads)
+    def _(h):
         scores = mm_t(keys[:, head(h)], queries[:, head(h)])
         top = jnp.max(scores, axis=1, keepdims=True)
         exps = jnp.exp(scores - top)
         exp_c[h] = exps.astype(BF16)
-        return put(h, stats, top, jnp.sum(exps, axis=1, keepdims=True))
-
-    def row_head(h, stats):
-        scores = jnp.where(mask, mm_t(queries[:, head(h)], keys[:, head(h)]), MASKED)
-        top = jnp.maximum(jnp.max(scores, axis=1, keepdims=True), FLOOR)
-        exps = jnp.exp(scores - top)
-        exp_r[h] = exps.astype(BF16)
-        return put(h, stats, top, jnp.sum(exps, axis=1, keepdims=True))
-
-    stats = over_heads(column_head, jnp.zeros((n_cols, 128), F32))
-    stat_c[my_img] = stats.T[: 2 * heads]
+        put(h, seen_c, top, jnp.sum(exps, axis=1, keepdims=True))
+
+    stat_c[my_img] = seen_c[...].T[: 2 * heads]
     send("img", lambda p: stat_c.at[my_img], stat_c, sc_s, sc_r)
+
     def factor(buf, mine):
         tops, sums = buf[:, :heads, :], buf[:, heads:, :]
         top = jnp.max(tops, axis=0)
@@ -234,20 +232,29 @@
         own = jnp.exp(buf[mine][:heads] - top) / total
         return jnp.concatenate([own, jnp.zeros((128 - heads, own.shape[1]), F32)], axis=0).T
 
-    def numerators(exps, values):
-        return [mm(exps[h], values[:, head(h)]) for h in range(heads)]
-
-    def update(numers, scale, out_weight):
-        delta = 0.0
-        for h in range(heads):
-            delta += mm((numers[h] * scale[:, h : h + 1]).astype(BF16), out_weight[head(h), :])
-        return delta
+    def update(numer, scale, out_weight, sums):
+        sums[...] = jnp.zeros(sums.shape, F32)
+
+        @pl.loop(0, heads)
+        def _(h):
+            own = jnp.sum(jnp.where(iota(scale.shape, 1) == h, scale, 0.0), axis=1, keepdims=True)
+            sums[...] += mm((numer[h] * own).astype(BF16), out_weight[head(h), :])
+
+        return sums[...]
 
     for p in beyond:
         project_values(p)
-    numers_p = numerators(exp_c, values_i)
+
+    @pl.loop(0, heads)
+    def _(h):
+        numer_p[h] = mm(exp_c[h], values_i[:, head(h)])
+
     loads[3].wait()
-    values_p[...] = mm(x_prompt, wvp[...]).astype(BF16)
+
+    @pl.loop(0, heads)
+    def _(h):
+        values_p[:, head(h)] = mm(x_prompt[...], wvp[:, head(h)]).astype(BF16)
+
     whole(meta, meta_s, meta_r).wait_recv()
     per = 128 // spare
     tall_marks = [jnp.sum(meta[g * 8 : g * 8 + 8, :, 128:256], axis=0) for g in range(n_img // 8)]
@@ -255,7 +262,7 @@
     mask = jnp.concatenate(tall_marks + short_marks, axis=1)[:, :n_cols] > 0
     loads[4].wait()
     whole(stat_c, sc_s, sc_r).wait_recv()
-    delta = update(numers_p, factor(stat_c, my_img), wop)
+    delta = update(numer_p, factor(stat_c, my_img), wop, sum_p)
     tall = delta[: n_img * TILE].reshape(n_img, TILE, width)
     short = delta[n_img * TILE :].reshape(n_img, spare, width)
     short = jnp.concatenate([short[:, :, :half], short[:, :, half:]], axis=1)
@@ -263,8 +270,15 @@
     dp_in[my_img] = dp_out[my_img]
     send("img", lambda p: dp_out.at[p], dp_in, dp_s, dp_r)
 
-    stats = over_heads(row_head, jnp.zeros((n_rows, 128), F32))
-    stat_r[my_txt] = stats.T[: 2 * heads]
+    @pl.loop(0, heads)
+    def _(h):
+        scores = jnp.where(mask, mm_t(queries[:, head(h)], keys[:, head(h)]), MASKED)
+        top = jnp.maximum(jnp.max(scores, axis=1, keepdims=True), FLOOR)
+        exps = jnp.exp(scores - top)
+        put(h, seen_r, top, jnp.sum(exps, axis=1, keepdims=True))
+        numer_i[h] = mm(exps.astype(BF16), values_p[:, head(h)])
+
+    stat_r[my_txt] = seen_r[...].T[: 2 * heads]
     send("txt", lambda p: stat_r.at[my_txt], stat_r, sr_s, sr_r)
 
     packed = jnp.concatenate([jnp.sum(meta[g * 8 : g * 8 + 8, :, :128], axis=0) for g in range(n_img // 8)], axis=1)
@@ -275,8 +289,6 @@
     numbers = jnp.broadcast_to((packed // COUNT_BASE).astype(F32), (8, n_img * 16)).astype(BF16)
     tally[my_txt] = mm_t(numbers, pick_lo)
     send("txt", lambda p: tally.at[my_txt], tally, tally_s, tally_r)
-
-    numers_i = numerators(exp_r, values_p)
 
     whole(dp_in, dp_s, dp_r).wait_recv()
     total = jnp.sum(dp_in[...].astype(F32), axis=0)
@@ -292,7 +304,7 @@
 
     loads[5].wait()
     whole(stat_r, sr_s, sr_r).wait_recv()
-    di_out[...] = update(numers_i, factor(stat_r, my_txt), woi).astype(BF16).reshape(di_out.shape)
+    di_out[...] = update(numer_i, factor(stat_r, my_txt), woi, sum_i).astype(BF16).reshape(di_out.shape)
     di_in[my_txt] = di_out[my_txt]
     send("txt", lambda p: di_out.at[p], di_in, di_s, di_r)
 
@@ -364,7 +376,13 @@
             pltpu.VMEM((n_rows, embed), BF16),
             pltpu.VMEM((n_cols, embed), BF16),
             pltpu.VMEM((heads, n_cols, n_rows), BF16),
-            pltpu.VMEM((heads, n_rows, n_cols), BF16),
+            pltpu.VMEM((n_cols, width), BF16),
+            pltpu.VMEM((n_cols, 128), F32),
+            pltpu.VMEM((n_rows, 128), F32),
+            pltpu.VMEM((heads, n_cols, HD), F32),
+            pltpu.VMEM((heads, n_rows, HD), F32),
+            pltpu.VMEM((n_cols, width), F32),
+            pltpu.VMEM((n_rows, width), F32),
             pltpu.VMEM((n_txt, 2 * heads, n_rows), F32),
             pltpu.VMEM((n_img, 2 * heads, n_cols), F32),
             pltpu.VMEM((n_txt, rows, width), BF16),

time: 31.6 us -> 34.8 us (1.10)
  Pallas kernels: 30.7 us -> 33.9 us
    pallas_call x1, Pallas kernels: 30.1 us -> 33.3 us  [on_device(): pl.pallas_call(functools.partial(kernel, n_img, n_txt), out_shape=tuple((...]
where the time goes in v6:
time: 34.8 us; the launch traced here: 34.6 us
  Pallas kernels  33.9 us (97%)
  between operations  0.64 us (2%)
    pallas_call x1, Pallas kernels, on_device(): pl.pallas_call(functools.partial(kernel, n_img, n_txt), out_shape=tuple((...  33.3 us

profile of v6, /device:TPU:0, one launch (start us, length us, event | category | flops | bytes accessed | tf_op | source)
XLA Modules:
  0.0 34.6 jit_solution(5106517636984933562)
XLA Ops:
  0.6 33.3 %joining_layer.1 = (bf16[128,256]{1,0:T(8,128)(2,1)S(1)}, bf16[24,256]{1,0:T(8,128)(2,1)S(1)}, f32[48,256]{1,0:T(8,128)S(1)}) custom-call(bf16[128,256]{1,0:T(8,128)(2,1)} %img_hbm.1, bf16[24,256]{1,0:T(8,128)(2,1)} %prompt_hbm.1, s32[24]{0:T(128)} %ids_hbm.1, s32[24]{0:T(128)} %valid_hbm.1, f32[256]{0:T(256)} %igain_hbm.1, f32[256]{0:T(256)} %pgain_hbm.1, ...), custom_call_target="tpu_custom_call" | custom-call | tf_op jit(solution)/shard_map/joining_layer/pallas_call | solution.py:362
  33.9 0.7 %keep.1 = (bf16[128,256]{1,0:T(8,128)(2,1)}, bf16[24,256]{1,0:T(8,128)(2,1)}, f32[48,256]{1,0:T(8,128)}) custom-call(bf16[128,256]{1,0:T(8,128)(2,1)S(1)} %get-tuple-element.6.refs_0_, bf16[24,256]{1,0:T(8,128)(2,1)S(1)} %get-tuple-element.7.refs_1_, f32[48,256]{1,0:T(8,128)S(1)} %get-tuple-element.8.refs_2_), custom_call_target="tpu_custom_call" | custom-call | tf_op jit(solution)/shard_map/keep/pallas_call | solution.py:407

commit v7 on v5

--- a/solution.py
+++ b/solution.py
@@ -51,7 +51,7 @@
     wq_hbm, wk_hbm, wvi_hbm, wvp_hbm, woi_hbm, wop_hbm, iscale_hbm, pscale_hbm,
     out_img, out_prompt, out_cat,
     img_ref, prompt_ref, ids_ref, valid_ref, igain_ref, pgain_ref, iscale_ref, pscale_ref,
-    wq, wk, wvi, wvp, woi, wop, xi, xp, meta, queries, keys, values_i, values_p, exp_c, exp_r,
+    wq, wk, wvi, wvp, woi, wop, xi, xp, meta, queries, keys, values_i, values_p, exp_c, exp_r, x_prompt,
     stat_r, stat_c, di_out, di_in, dp_out, dp_in, win, tally, cat,
     in_sem, w_sem, xi_s, xi_r, relay_s, xp_s, xp_r, meta_s, meta_r, sr_s, sr_r, sc_s, sc_r,
     di_s, di_r, dp_s, dp_r, win_s, win_r, tally_s, tally_r, cat_s, cat_r,
@@ -156,45 +156,41 @@
     image_copy(mate, my_txt).start()
     send("img", lambda p: meta.at[my_img], meta, meta_s, meta_r)
 
-    def image_rows(p):
-        return pl.ds(pl.multiple_of(p * rows, rows), rows)
-
-    def project_queries(p):
-        queries[image_rows(p), :] = (mm(xi[p], wq[...]) * (HD ** -0.5)).astype(BF16)
-
-    def project_values(p):
-        values_i[image_rows(p), :] = mm(xi[p], wvi[...]).astype(BF16)
-
     def relay(p):
         return pltpu.make_async_remote_copy(
             xi.at[p], xi.at[p], relay_s.at[p], xi_r.at[p], device_id=place("txt", mate), device_id_type=MESH
         )
 
-    loads[0].wait()
-    project_queries(my_txt)
     for p in far:
         image_copy(p, p).wait_recv()
         relay(p).start()
-    loads[1].wait()
-    project_values(my_txt)
-    image_copy(mate, mate).wait_recv()
-    project_queries(mate)
-    project_values(mate)
-    for p in far:
-        project_queries(p)
-        project_values(p)
+    for load in loads[:4]:
+        load.wait()
+
+    def lanes(h):
+        return pl.ds(pl.multiple_of(h * HD, HD), HD)
 
     whole(xp, xp_s, xp_r).wait_recv()
     tall = xp[:, :, :width].reshape(n_img * TILE, width)
     short = xp[:, :, width:].astype(F32)
     short = jnp.concatenate([short[:, :spare], short[:, spare:]], axis=2).reshape(n_img * spare, width)
-    x_prompt = jnp.concatenate([tall, short.astype(BF16)], axis=0)
-    loads[2].wait()
-    keys[...] = mm(x_prompt, wk[...]).astype(BF16)
-    beyond = [p + 1 - 2 * (p % 2) for p in far]
-    for p in beyond:
-        image_copy(p, p).wait_recv()
-        project_queries(p)
+    x_prompt[...] = jnp.concatenate([tall, short.astype(BF16)], axis=0)
+
+    @pl.loop(0, heads)
+    def _(h):
+        keys[:, lanes(h)] = mm(x_prompt[...], wk[:, lanes(h)]).astype(BF16)
+        values_p[:, lanes(h)] = mm(x_prompt[...], wvp[:, lanes(h)]).astype(BF16)
+
+    image_copy(mate, mate).wait_recv()
+    for p in far:
+        beyond = p + 1 - 2 * (p % 2)
+        image_copy(beyond, beyond).wait_recv()
+
+    @pl.loop(0, heads)
+    def _(h):
+        x_image = xi[...].reshape(n_rows, width)
+        queries[:, lanes(h)] = (mm(x_image, wq[:, lanes(h)]) * (HD ** -0.5)).astype(BF16)
+        values_i[:, lanes(h)] = mm(x_image, wvi[:, lanes(h)]).astype(BF16)
 
     def over_heads(body, stats):
         if n_cols <= 512:
@@ -243,11 +239,7 @@
             delta += mm((numers[h] * scale[:, h : h + 1]).astype(BF16), out_weight[head(h), :])
         return delta
 
-    for p in beyond:
-        project_values(p)
     numers_p = numerators(exp_c, values_i)
-    loads[3].wait()
-    values_p[...] = mm(x_prompt, wvp[...]).astype(BF16)
     whole(meta, meta_s, meta_r).wait_recv()
     per = 128 // spare
     tall_marks = [jnp.sum(meta[g * 8 : g * 8 + 8, :, 128:256], axis=0) for g in range(n_img // 8)]
@@ -365,6 +357,7 @@
             pltpu.VMEM((n_cols, embed), BF16),
             pltpu.VMEM((heads, n_cols, n_rows), BF16),
             pltpu.VMEM((heads, n_rows, n_cols), BF16),
+            pltpu.VMEM((n_cols, width), BF16),
             pltpu.VMEM((n_txt, 2 * heads, n_rows), F32),
             pltpu.VMEM((n_img, 2 * heads, n_cols), F32),
             pltpu.VMEM((n_txt, rows, width), BF16),

time: 31.6 us -> 33.1 us (1.047)
  Pallas kernels: 30.7 us -> 32.2 us
    pallas_call x1, Pallas kernels: 30.1 us -> 31.6 us  [on_device(): pl.pallas_call(functools.partial(kernel, n_img, n_txt), out_shape=tuple((...]
where the time goes in v7:
time: 33.1 us; the launch traced here: 32.9 us
  Pallas kernels  32.2 us (97%)
  between operations  0.64 us (2%)
    pallas_call x1, Pallas kernels, on_device(): pl.pallas_call(functools.partial(kernel, n_img, n_txt), out_shape=tuple((...  31.6 us

profile of v7, /device:TPU:0, one launch (start us, length us, event | category | flops | bytes accessed | tf_op | source)
XLA Modules:
  0.0 32.9 jit_solution(4342641892427324786)
XLA Ops:
  0.6 31.6 %joining_layer.1 = (bf16[128,256]{1,0:T(8,128)(2,1)S(1)}, bf16[24,256]{1,0:T(8,128)(2,1)S(1)}, f32[48,256]{1,0:T(8,128)S(1)}) custom-call(bf16[128,256]{1,0:T(8,128)(2,1)} %img_hbm.1, bf16[24,256]{1,0:T(8,128)(2,1)} %prompt_hbm.1, s32[24]{0:T(128)} %ids_hbm.1, s32[24]{0:T(128)} %valid_hbm.1, f32[256]{0:T(256)} %igain_hbm.1, f32[256]{0:T(256)} %pgain_hbm.1, ...), custom_call_target="tpu_custom_call" | custom-call | tf_op jit(solution)/shard_map/joining_layer/pallas_call | solution.py:342
  32.2 0.7 %keep.1 = (bf16[128,256]{1,0:T(8,128)(2,1)}, bf16[24,256]{1,0:T(8,128)(2,1)}, f32[48,256]{1,0:T(8,128)}) custom-call(bf16[128,256]{1,0:T(8,128)(2,1)S(1)} %get-tuple-element.6.refs_0_, bf16[24,256]{1,0:T(8,128)(2,1)S(1)} %get-tuple-element.7.refs_1_, f32[48,256]{1,0:T(8,128)S(1)} %get-tuple-element.8.refs_2_), custom_call_target="tpu_custom_call" | custom-call | tf_op jit(solution)/shard_map/keep/pallas_call | solution.py:382

commit v8 on v5

--- a/solution.py
+++ b/solution.py
@@ -196,12 +196,12 @@
         image_copy(p, p).wait_recv()
         project_queries(p)
 
-    def over_heads(body, stats):
+    def over_heads(body, stats, first=0, last=heads):
         if n_cols <= 512:
-            for h in range(heads):
+            for h in range(first, last):
                 stats = body(h, stats)
             return stats
-        return lax.fori_loop(0, heads, body, stats)
+        return lax.fori_loop(first, last, body, stats)
 
     def head(h):
         return pl.ds(h * HD, HD) if isinstance(h, int) else pl.ds(pl.multiple_of(h * HD, HD), HD)
@@ -253,6 +253,7 @@
     tall_marks = [jnp.sum(meta[g * 8 : g * 8 + 8, :, 128:256], axis=0) for g in range(n_img // 8)]
     short_marks = [jnp.sum(meta[g : min(g + per, n_img), :, 256:], axis=0) for g in range(0, n_img, per)]
     mask = jnp.concatenate(tall_marks + short_marks, axis=1)[:, :n_cols] > 0
+    row_stats = over_heads(row_head, jnp.zeros((n_rows, 128), F32), 0, heads // 2)
     loads[4].wait()
     whole(stat_c, sc_s, sc_r).wait_recv()
     delta = update(numers_p, factor(stat_c, my_img), wop)
@@ -263,8 +264,8 @@
     dp_in[my_img] = dp_out[my_img]
     send("img", lambda p: dp_out.at[p], dp_in, dp_s, dp_r)
 
-    stats = over_heads(row_head, jnp.zeros((n_rows, 128), F32))
-    stat_r[my_txt] = stats.T[: 2 * heads]
+    row_stats = over_heads(row_head, row_stats, heads // 2, heads)
+    stat_r[my_txt] = row_stats.T[: 2 * heads]
     send("txt", lambda p: stat_r.at[my_txt], stat_r, sr_s, sr_r)
 
     packed = jnp.concatenate([jnp.sum(meta[g * 8 : g * 8 + 8, :, :128], axis=0) for g in range(n_img // 8)], axis=1)
@@ -275,8 +276,6 @@
     numbers = jnp.broadcast_to((packed // COUNT_BASE).astype(F32), (8, n_img * 16)).astype(BF16)
     tally[my_txt] = mm_t(numbers, pick_lo)
     send("txt", lambda p: tally.at[my_txt], tally, tally_s, tally_r)
-
-    numers_i = numerators(exp_r, values_p)
 
     whole(dp_in, dp_s, dp_r).wait_recv()
     total = jnp.sum(dp_in[...].astype(F32), axis=0)
@@ -290,6 +289,7 @@
     send("img", lambda p: win.at[my_img], win, win_s, win_r)
     out_prompt[...] = joined.astype(BF16)
 
+    numers_i = numerators(exp_r, values_p)
     loads[5].wait()
     whole(stat_r, sr_s, sr_r).wait_recv()
     di_out[...] = update(numers_i, factor(stat_r, my_txt), woi).astype(BF16).reshape(di_out.shape)

time: 31.6 us -> 31.6 us (level)
  no operation moved by 1% of the time
where the time goes in v8:
time: 31.6 us; the launch traced here: 31.4 us
  Pallas kernels  30.7 us (97%)
  between operations  0.64 us (2%)
    pallas_call x1, Pallas kernels, on_device(): pl.pallas_call(functools.partial(kernel, n_img, n_txt), out_shape=tuple((...  30.1 us
    pallas_call x1, Pallas kernels, on_device(): pl.pallas_call(keep, out_shape=outs, in_specs=[vmem] * len(outs), out_spe...  0.66 us

profile of v8, /device:TPU:0, one launch (start us, length us, event | category | flops | bytes accessed | tf_op | source)
XLA Modules:
  0.0 31.4 jit_solution(15716415136853445949)
XLA Ops:
  0.6 30.1 %joining_layer.1 = (bf16[128,256]{1,0:T(8,128)(2,1)S(1)}, bf16[24,256]{1,0:T(8,128)(2,1)S(1)}, f32[48,256]{1,0:T(8,128)S(1)}) custom-call(bf16[128,256]{1,0:T(8,128)(2,1)} %img_hbm.1, bf16[24,256]{1,0:T(8,128)(2,1)} %prompt_hbm.1, s32[24]{0:T(128)} %ids_hbm.1, s32[24]{0:T(128)} %valid_hbm.1, f32[256]{0:T(256)} %igain_hbm.1, f32[256]{0:T(256)} %pgain_hbm.1, ...), custom_call_target="tpu_custom_call" | custom-call | tf_op jit(solution)/shard_map/joining_layer/pallas_call | solution.py:350
  30.7 0.7 %keep.1 = (bf16[128,256]{1,0:T(8,128)(2,1)}, bf16[24,256]{1,0:T(8,128)(2,1)}, f32[48,256]{1,0:T(8,128)}) custom-call(bf16[128,256]{1,0:T(8,128)(2,1)S(1)} %get-tuple-element.6.refs_0_, bf16[24,256]{1,0:T(8,128)(2,1)S(1)} %get-tuple-element.7.refs_1_, f32[48,256]{1,0:T(8,128)S(1)} %get-tuple-element.8.refs_2_), custom_call_target="tpu_custom_call" | custom-call | tf_op jit(solution)/shard_map/keep/pallas_call | solution.py:389
